TPU v7x, 32 devices: a whole 2x2x4 slice. The times are simulated.
32 devices in a mesh: dp: 4 (over z), ctx: 8 (over y, x, core).
Axes of the slice: x: 2, y: 2, z: 4, core: 2. Of those that a mesh axis runs over, the one named last changes fastest.
Arguments:
- q_proj: bfloat16 [4, 1024, 3072], P('dp', 'ctx'), may hold values from -6 to 6
- k_proj: bfloat16 [4, 1024, 512], P('dp', 'ctx'), may hold values from -6 to 6
- v_proj: bfloat16 [4, 1024, 512], P('dp', 'ctx'), may hold values from -6 to 6
- out_grad: bfloat16 [4, 1024, 3072], P('dp', 'ctx'), may hold values from -6 to 6
- q_gain: float32 [128], replicated, may hold values from 0.1 to 1.9
- k_gain: float32 [128], replicated, may hold values from 0.1 to 1.9
- pos_ids: int32 [4, 3, 1024], P('dp', None, 'ctx'), may hold values from 0 to 63
- stretch_lengths: int32 [4, 32], P('dp'), may hold values from 1 to 64, 1024 in all within a row
- stretch_windows: int32 [4, 32], P('dp'), may hold values from 0 to 1
- clip_ids: int32 [4, 32], P('dp'), may hold values from 0 to 7, never falling along the last dimension, each value on 1 to 8 neighbouring positions
- dispatch_plan: int32 [4, 8], P('dp'), may hold values from 0 to 7, as said below
Outputs:
- q_grad: bfloat16 [4, 1024, 3072], P('dp', 'ctx')
- k_grad: bfloat16 [4, 1024, 512], P('dp', 'ctx')
- v_grad: bfloat16 [4, 1024, 512], P('dp', 'ctx')
- q_gain_grad: float32 [128], replicated
- k_gain_grad: float32 [128], replicated
Inputs may be any that keep to these rules, and one draw needn't show every extreme that they name: In each batch every block number appears once, and a slot holds a block of its own aligned pair of devices: dispatch_plan[s] // 2 == s // 2. `stretch_lengths`: in each batch the lengths sum to 1024, and the longest is exactly 64. `clip_ids`: never falls along a batch's stretches; each clip has 1 to 8 stretches, one exactly 8.
All inputs are finite; a program needn't handle non-finite values.
Results may differ from a plain program's by a relative error of at most 0.013.
Values may be sent and summed in bfloat16 or wider, within the bound.
A program may use at most 64 MiB of HBM per device.

v0:
```python
import functools
import math

import jax
import jax.numpy as jnp
from jax import lax
from jax.experimental import pallas as pl
from jax.experimental.pallas import tpu as pltpu
from jax.sharding import PartitionSpec as P

MESH = pl.DeviceIdType.MESH
F32 = jnp.float32
BF16 = jnp.bfloat16
BLOCK = 128
HALF = BLOCK // 2
SPAN = 2 * BLOCK + HALF
norm_eps = 1e-06
VMEM_LIMIT = 60 * 1024 * 1024
rope_base = 10000.0

NT = (((1,), (1,)), ((), ()))
TN = (((0,), (0,)), ((), ()))


def sin_cos(angle):
    turns = jnp.floor(angle * (2.0 / math.pi) + 0.5)
    rest = angle - turns * 1.5703125
    rest = rest - turns * 4.837512969970703125e-4
    rest = rest - turns * 7.549789948768648e-8
    square = rest * rest
    sine = rest + rest * square * (
        -1.6666654611e-1 + square * (8.3321608736e-3 + square * -1.9515295891e-4)
    )
    cosine = (
        1.0
        - 0.5 * square
        + square
        * square
        * (4.166664568298827e-2 + square * (-1.388731625493765e-3 + square * 2.443315711809948e-5))
    )
    quarter = turns.astype(jnp.int32)
    odd = (quarter & 1) == 1
    sine_out = jnp.where(odd, cosine, sine)
    cosine_out = jnp.where(odd, sine, cosine)
    sine_out = jnp.where((quarter & 2) == 2, -sine_out, sine_out)
    cosine_out = jnp.where(((quarter + 1) & 2) == 2, -cosine_out, cosine_out)
    return sine_out, cosine_out


def roll_half(x):
    return pltpu.roll(x, HALF, 1)


def rope_tables(ids):
    rows = lax.broadcasted_iota(jnp.int32, (BLOCK, BLOCK), 0)
    lanes = lax.broadcasted_iota(jnp.int32, (BLOCK, BLOCK), 1)
    columns = [
        jnp.sum(jnp.where(rows == lanes, ids[t].astype(F32), 0.0), axis=1, keepdims=True)
        for t in range(3)
    ]
    pair = lanes % HALF
    chosen = jnp.where(pair < 16, columns[0], jnp.where(pair < 40, columns[1], columns[2]))
    pair_row = lax.broadcasted_iota(jnp.int32, (1, BLOCK), 1) % HALF
    frequency = jnp.exp(pair_row.astype(F32) * (-math.log(rope_base) / HALF))
    sine, cosine = sin_cos(chosen * frequency)
    return cosine, jnp.where(lanes < HALF, -sine, sine)


def key_ranges(lengths, windows, clips, start):
    count = lengths.shape[1]
    rows = lax.broadcasted_iota(jnp.int32, (count, count), 0)
    lanes = lax.broadcasted_iota(jnp.int32, (count, count), 1)

    def column(where_, values):
        return jnp.sum(jnp.where(where_, values.astype(F32), 0.0), axis=1, keepdims=True)

    ends = column(lanes <= rows, lengths)
    starts = column(lanes < rows, lengths)
    before = column(lanes == rows - 1, lengths)
    window = column(lanes == rows, windows)
    clip = column(lanes == rows, clips + 1)
    clip_before = column(lanes == rows - 1, clips + 1)
    low = starts - jnp.where(clip == clip_before, window * before, 0.0)
    spots = (start + lax.broadcasted_iota(jnp.int32, (count, BLOCK), 1)).astype(F32)
    inside = (starts <= spots) & (spots < ends)
    low_row = jnp.sum(jnp.where(inside, low, 0.0), axis=0, keepdims=True)
    high_row = jnp.sum(jnp.where(inside, ends, 0.0), axis=0, keepdims=True)
    return low_row, high_row


def kernel(
    n,
    n_dp,
    groups,
    per_group,
    plan_hbm,
    k_hbm,
    v_hbm,
    qg_hbm,
    kg_hbm,
    ids_hbm,
    len_hbm,
    win_hbm,
    clip_hbm,
    q_hbm,
    do_hbm,
    qgrad_hbm,
    kgrad_hbm,
    vgrad_hbm,
    qgain_hbm,
    kgain_hbm,
    plan_ref,
    k_ref,
    v_ref,
    qg_ref,
    kg_ref,
    ids_ref,
    len_ref,
    win_ref,
    clip_ref,
    q_vm,
    do_vm,
    qout,
    kgrad_ref,
    vgrad_ref,
    gain_ref,
    qrot,
    qinv,
    dq,
    own,
    other,
    to_prev,
    to_next,
    from_prev,
    from_next,
    parts,
    back_prev,
    back_next,
    back,
    met,
    home_prev,
    home_next,
    back_pair,
    home_pair,
    term_ctx,
    term_dp,
    load_sem,
    out_sem,
    pair_s,
    pair_r,
    np_s,
    np_r,
    nn_s,
    nn_r,
    bp_s,
    bp_r,
    bn_s,
    bn_r,
    hp_s,
    hp_r,
    fp_s,
    fp_r,
    fn_s,
    fn_r,
    mt_s,
    mt_r,
    tc_s,
    tc_r,
    td_s,
    td_r,
):
    me = lax.axis_index("ctx")
    dp = lax.axis_index("dp")
    partner = me + 1 - 2 * lax.rem(me, 2)
    has_prev = me >= 2
    has_next = me < n - 2
    width = per_group * BLOCK
    inv_sqrt = BLOCK ** (-0.5)

    sources = (
        ids_hbm, kg_hbm, k_hbm, v_hbm, plan_hbm, qg_hbm, len_hbm, win_hbm, clip_hbm, q_hbm, do_hbm
    )
    targets = (
        ids_ref, kg_ref, k_ref, v_ref, plan_ref, qg_ref, len_ref, win_ref, clip_ref, q_vm, do_vm
    )
    loads = [
        pltpu.make_async_copy(source, target, load_sem.at[i])
        for i, (source, target) in enumerate(zip(sources, targets))
    ]
    for load in loads:
        load.start()

    barrier = pltpu.get_barrier_semaphore()

    def greet_ctx(step, carry):
        peer = lax.rem(me + step, n)
        pl.semaphore_signal(barrier, inc=1, device_id=(dp, peer), device_id_type=MESH)
        return carry

    def greet_dp(step, carry):
        peer = lax.rem(dp + step, n_dp)
        pl.semaphore_signal(barrier, inc=1, device_id=(peer, me), device_id_type=MESH)
        return carry

    for g in range(groups):
        edge = lax.rem(me, 2) != g // (groups // 2)

        @pl.when(jnp.logical_or(edge, jnp.logical_not(has_prev)))
        def _():
            home_prev[g] = jnp.zeros_like(home_prev[g])

        @pl.when(jnp.logical_or(edge, jnp.logical_not(has_next)))
        def _():
            home_next[g] = jnp.zeros_like(home_next[g])

    @pl.when(jnp.logical_not(has_prev))
    def _():
        from_prev[...] = jnp.zeros_like(from_prev)

    @pl.when(jnp.logical_not(has_next))
    def _():
        from_next[...] = jnp.zeros_like(from_next)

    lax.fori_loop(1, n, greet_ctx, 0)
    lax.fori_loop(1, n_dp, greet_dp, 0)

    def remote(source, target, send, receive, peer):
        return pltpu.make_async_remote_copy(
            src_ref=source,
            dst_ref=target,
            send_sem=send,
            recv_sem=receive,
            device_id=peer,
            device_id_type=MESH,
        )

    for load in loads[:9]:
        load.wait()
    block = plan_ref[0, me]
    is_odd = lax.rem(block, 2) == 1

    cosine, sine = rope_tables(ids_ref)
    k_gain = kg_ref[...]
    q_gain = qg_ref[...]
    kc, ks = cosine * k_gain, sine * roll_half(k_gain)
    k_inv = []
    for g in range(groups):
        x = k_ref[0, :, g * BLOCK : (g + 1) * BLOCK].astype(F32)
        inv = lax.rsqrt(jnp.mean(x * x, axis=1, keepdims=True) + norm_eps)
        own[g, :, :BLOCK] = (inv * (x * kc + roll_half(x) * ks)).astype(BF16)
        own[g, :, BLOCK:] = v_ref[0, :, g * BLOCK : (g + 1) * BLOCK]

    pl.semaphore_wait(barrier, n - 1 + n_dp - 1)

    pair = [
        remote(own.at[g], other.at[g], pair_s.at[g], pair_r.at[g], (dp, partner))
        for g in range(groups)
    ]
    order = [g for i in range(groups // 2) for g in (i, i + groups // 2)]
    for g in order:
        pair[g].start()

    low_row, high_row = key_ranges(len_ref[...], win_ref[...], clip_ref[...], block * BLOCK)
    spots = ((block - 1) * BLOCK + lax.broadcasted_iota(jnp.int32, (SPAN, BLOCK), 0)).astype(F32)
    bias = jnp.where((spots >= low_row) & (spots < high_row), 0.0, -1e30)
    bias = jnp.concatenate([bias, bias], axis=1)

    qc, qs = cosine * q_gain, sine * roll_half(q_gain)
    loads[9].wait()

    def rotate_group(g):
        for j in range(per_group):
            h = g * per_group + j
            x = q_vm[0, :, h * BLOCK : (h + 1) * BLOCK].astype(F32)
            inv = lax.rsqrt(jnp.mean(x * x, axis=1, keepdims=True) + norm_eps)
            qinv[h] = inv
            qrot[g, j * BLOCK : (j + 1) * BLOCK, :] = (inv * (x * qc + roll_half(x) * qs)).astype(
                BF16
            )

    send_prev = [
        remote(to_prev.at[g], from_next.at[g], np_s.at[g], nn_r.at[g], (dp, me - 2))
        for g in range(groups)
    ]
    send_next = [
        remote(to_next.at[g], from_prev.at[g], nn_s.at[g], np_r.at[g], (dp, me + 2))
        for g in range(groups)
    ]
    pass_prev = [
        remote(from_prev.at[g], from_prev.at[g], fp_s.at[g], fp_r.at[g], (dp, partner))
        for g in range(groups)
    ]
    pass_next = [
        remote(from_next.at[g], from_next.at[g], fn_s.at[g], fn_r.at[g], (dp, partner))
        for g in range(groups)
    ]
    share = groups // 2
    core = lax.rem(me, 2)

    def mine(g):
        return core == g // share

    def both(one, two):
        return jnp.logical_and(one, two)

    for g in order:
        pair[g].wait_recv()

        @pl.when(mine(g))
        def _():
            own_g, other_g = own[g], other[g]
            to_next[g] = lax.select(is_odd, own_g, other_g)
            to_prev[g] = lax.select(is_odd, other_g[:HALF], own_g[:HALF])

        @pl.when(both(has_next, mine(g)))
        def _():
            send_next[g].start()

        @pl.when(both(has_prev, mine(g)))
        def _():
            send_prev[g].start()

    for g in range(groups):
        rotate_group(g)
    loads[10].wait()

    return_prev = [
        remote(back_prev.at[g], home_next.at[g], bp_s.at[g], bn_r.at[g], (dp, me - 2))
        for g in range(groups)
    ]
    return_next = [
        remote(back_next.at[g], home_prev.at[g], bn_s.at[g], bp_r.at[g], (dp, me + 2))
        for g in range(groups)
    ]
    scale = inv_sqrt * math.log2(math.e)
    def pass_on(g):
        @pl.when(both(has_prev, mine(g)))
        def _():
            send_next[g].wait_recv()
            pass_prev[g].start()

        @pl.when(both(has_next, mine(g)))
        def _():
            send_prev[g].wait_recv()
            pass_next[g].start()

    def send_back(g):
        @pl.when(mine(g))
        def _():
            meet[g].wait_recv()
            back_prev[g] = back[g, :BLOCK] + met[g, :BLOCK]
            back_next[g] = back[g, BLOCK:] + met[g, BLOCK:]

        @pl.when(both(has_prev, mine(g)))
        def _():
            return_prev[g].start()

        @pl.when(both(has_next, mine(g)))
        def _():
            return_next[g].start()

    meet = [
        remote(back.at[g], met.at[g], mt_s.at[g], mt_r.at[g], (dp, partner))
        for g in range(groups)
    ]
    for place, g in enumerate(order):
        if place % 2 == 0:
            pass_on(order[place])
            pass_on(order[place + 1])

        @pl.when(both(has_prev, jnp.logical_not(mine(g))))
        def _():
            pass_prev[g].wait_recv()

        @pl.when(both(has_next, jnp.logical_not(mine(g))))
        def _():
            pass_next[g].wait_recv()

        other_g = other[g]
        keys = jnp.concatenate(
            [
                lax.select(is_odd, other_g, from_prev[g]),
                own[g],
                lax.select(is_odd, from_next[g], other_g[:HALF]),
            ],
            axis=0,
        )
        key, value = keys[:, :BLOCK], keys[:, BLOCK:]
        prob_list, grad_list = [], []
        for j in range(per_group // 2):
            first = g * per_group + 2 * j
            query = qrot[g, 2 * j * BLOCK : (2 * j + 2) * BLOCK, :]
            cot = jnp.concatenate(
                [
                    do_vm[0, :, first * BLOCK : (first + 1) * BLOCK],
                    do_vm[0, :, (first + 1) * BLOCK : (first + 2) * BLOCK],
                ],
                axis=0,
            )
            scores = lax.dot_general(key, query, NT, preferred_element_type=F32)
            prob_grad = lax.dot_general(value, cot, NT, preferred_element_type=F32)
            weights = jnp.exp2(scores * scale + bias)
            inverse = 1.0 / jnp.sum(weights, axis=0, keepdims=True)
            delta = jnp.sum(weights * prob_grad, axis=0, keepdims=True) * inverse
            probs = weights * inverse
            prob_list.append(probs.astype(BF16))
            grad_list.append((probs * (prob_grad - delta)).astype(BF16))
        probs_low = jnp.concatenate(prob_list, axis=1)
        score_grad = jnp.concatenate(grad_list, axis=1)
        cots = jnp.concatenate(
            [
                do_vm[0, :, h * BLOCK : (h + 1) * BLOCK]
                for h in range(g * per_group, (g + 1) * per_group)
            ],
            axis=0,
        )
        parts[g, :, :BLOCK] = jnp.dot(score_grad, qrot[g], preferred_element_type=F32) * inv_sqrt
        parts[g, :, BLOCK:] = jnp.dot(probs_low, cots, preferred_element_type=F32)
        back[g, :BLOCK] = lax.select(
            is_odd, jnp.zeros((BLOCK, 2 * BLOCK), F32), parts[g, :BLOCK]
        ).astype(BF16)
        back[g, BLOCK:] = lax.select(
            is_odd, parts[g, 2 * BLOCK :], jnp.zeros((HALF, 2 * BLOCK), F32)
        ).astype(BF16)

        @pl.when(jnp.logical_not(mine(g)))
        def _():
            meet[g].start()

        if place % 2 == 0 and place >= 2:
            send_back(order[place - 2])
            send_back(order[place - 1])
        dq[g] = lax.dot_general(score_grad, key, TN, preferred_element_type=F32)

    send_back(order[-2])
    send_back(order[-1])
    cos_back, sin_back = cosine * inv_sqrt, sine * inv_sqrt
    q_term = jnp.zeros((BLOCK, BLOCK), F32)
    outs = []
    for g in range(groups):
        for j in range(per_group):
            h = g * per_group + j
            grad = dq[g, j * BLOCK : (j + 1) * BLOCK, :]
            inv = qinv[h]
            unit = q_vm[0, :, h * BLOCK : (h + 1) * BLOCK].astype(F32) * inv
            turned = grad * cos_back - roll_half(grad) * sin_back
            product = turned * unit
            q_term = q_term + product
            mean = jnp.mean(product * q_gain, axis=1, keepdims=True)
            qout[:, h * BLOCK : (h + 1) * BLOCK] = (inv * (turned * q_gain - unit * mean)).astype(
                BF16
            )
        columns = pl.ds(g * width, width)
        outs.append(
            pltpu.make_async_copy(qout.at[:, columns], qgrad_hbm.at[0, :, columns], out_sem.at[g])
        )
        outs[g].start()

    home = [
        remote(back_pair.at[g], home_pair.at[g], hp_s.at[g], hp_r.at[g], (dp, partner))
        for g in range(groups)
    ]
    for g in order:

        @pl.when(both(has_next, mine(g)))
        def _():
            return_prev[g].wait_recv()

        @pl.when(both(has_prev, mine(g)))
        def _():
            return_next[g].wait_recv()

        odd_in = home_next[g].astype(F32)
        even_in = home_prev[g].astype(F32)
        before, centre, after = parts[g, :BLOCK], parts[g, BLOCK : 2 * BLOCK], parts[g, 2 * BLOCK :]
        back_pair[g, :HALF] = lax.select(
            is_odd, before[:HALF] + even_in, after + odd_in[:HALF]
        ).astype(BF16)
        back_pair[g, HALF:] = lax.select(is_odd, before[HALF:], odd_in[HALF:]).astype(BF16)
        home[g].start()
        parts[g, BLOCK : BLOCK + HALF] = centre[:HALF] + lax.select(is_odd, odd_in[:HALF], even_in)
        parts[g, BLOCK + HALF : 2 * BLOCK] = centre[HALF:] + lax.select(
            is_odd, odd_in[HALF:], jnp.zeros((HALF, 2 * BLOCK), F32)
        )

    k_term = jnp.zeros((BLOCK, BLOCK), F32)
    for g in range(groups):
        home[g].wait_recv()
        total = parts[g, BLOCK : 2 * BLOCK] + home_pair[g].astype(F32)
        columns = slice(g * BLOCK, (g + 1) * BLOCK)
        vgrad_ref[0, :, columns] = total[:, BLOCK:].astype(BF16)
        grad = total[:, :BLOCK]
        x = k_ref[0, :, columns].astype(F32)
        inv = lax.rsqrt(jnp.mean(x * x, axis=1, keepdims=True) + norm_eps)
        unit = x * inv
        turned = grad * cosine - roll_half(grad) * sine
        product = turned * unit
        k_term = k_term + product
        mean = jnp.mean(product * k_gain, axis=1, keepdims=True)
        kgrad_ref[0, :, columns] = (inv * (turned * k_gain - unit * mean)).astype(BF16)
    outs.append(pltpu.make_async_copy(kgrad_ref, kgrad_hbm, out_sem.at[groups]))
    outs.append(pltpu.make_async_copy(vgrad_ref, vgrad_hbm, out_sem.at[groups + 1]))
    outs[groups].start()
    outs[groups + 1].start()

    term_ctx[me, 0:1] = jnp.sum(q_term, axis=0, keepdims=True)
    term_ctx[me, 1:2] = jnp.sum(k_term, axis=0, keepdims=True)

    def ctx_copy(step):
        peer = lax.rem(me + step, n)
        return remote(
            term_ctx.at[me], term_ctx.at[me], tc_s.at[step], tc_r.at[step], (dp, peer)
        )

    def dp_copy(step):
        peer = lax.rem(dp + step, n_dp)
        return remote(term_dp.at[dp], term_dp.at[dp], td_s.at[step], td_r.at[step], (peer, me))

    def run(copy_of, method):
        def body(step, carry):
            getattr(copy_of(step), method)()
            return carry

        return body

    lax.fori_loop(1, n, run(ctx_copy, "start"), 0)
    lax.fori_loop(1, n, run(ctx_copy, "wait_recv"), 0)
    term_dp[dp, 0:2] = jnp.sum(term_ctx[:, 0:2], axis=0)
    lax.fori_loop(1, n_dp, run(dp_copy, "start"), 0)

    for g in range(groups):
        pair[g].wait_send()
        home[g].wait_send()

        @pl.when(jnp.logical_not(mine(g)))
        def _():
            meet[g].wait_send()

        @pl.when(both(has_next, mine(g)))
        def _():
            send_next[g].wait_send()
            return_next[g].wait_send()
            pass_next[g].wait_send()

        @pl.when(both(has_prev, mine(g)))
        def _():
            send_prev[g].wait_send()
            return_prev[g].wait_send()
            pass_prev[g].wait_send()

    lax.fori_loop(1, n, run(ctx_copy, "wait_send"), 0)
    lax.fori_loop(1, n_dp, run(dp_copy, "wait_recv"), 0)
    sums = jnp.sum(term_dp[:, 0:2], axis=0)
    token_count = n_dp * n * BLOCK
    gain_ref[0] = sums[0:1] * (1.0 / math.sqrt(token_count * groups * per_group))
    gain_ref[1] = sums[1:2] * (1.0 / math.sqrt(token_count * groups))
    outs.append(pltpu.make_async_copy(gain_ref.at[0], qgain_hbm, out_sem.at[groups + 2]))
    outs.append(pltpu.make_async_copy(gain_ref.at[1], kgain_hbm, out_sem.at[groups + 3]))
    outs[groups + 2].start()
    outs[groups + 3].start()
    lax.fori_loop(1, n_dp, run(dp_copy, "wait_send"), 0)
    for out in outs:
        out.wait()


def hand_over(*refs):
    count = (len(refs) - 2) // 3
    sources, targets, middles = refs[:count], refs[count : 2 * count], refs[2 * count : -2]
    arrive, leave = refs[-2:]
    pieces = []
    for source, target, middle in zip(sources, targets, middles):
        if len(source.shape) == 3 and source.shape[2] >= 1024:
            rows = source.shape[1] // 4
            spots = [(0, slice(i * rows, (i + 1) * rows)) for i in range(4)]
        else:
            spots = [(slice(None),)]
        pieces += [(source.at[spot], middle.at[spot], target.at[spot]) for spot in spots]
    first = [
        pltpu.make_async_copy(source, middle, arrive.at[i])
        for i, (source, middle, target) in enumerate(pieces)
    ]
    second = [
        pltpu.make_async_copy(middle, target, leave.at[i])
        for i, (source, middle, target) in enumerate(pieces)
    ]
    for copy in first:
        copy.start()
    for copy, later in zip(first, second):
        copy.wait()
        later.start()
    for later in second:
        later.wait()


def shards(
    q_proj,
    k_proj,
    v_proj,
    out_grad,
    q_gain,
    k_gain,
    pos_ids,
    stretch_lengths,
    stretch_windows,
    clip_ids,
    dispatch_plan,
):
    n = lax.axis_size("ctx")
    n_dp = lax.axis_size("dp")
    groups = k_proj.shape[2] // BLOCK
    heads = q_proj.shape[2] // BLOCK
    per_group = heads // groups
    hbm = pl.BlockSpec(memory_space=pl.ANY)
    dma = pltpu.SemaphoreType.DMA
    whole = pltpu.VMEM((groups, BLOCK, 2 * BLOCK), BF16)
    half = pltpu.VMEM((groups, HALF, 2 * BLOCK), BF16)
    count = stretch_lengths.shape[1]
    shapes = (
        jax.ShapeDtypeStruct(q_proj.shape, BF16),
        jax.ShapeDtypeStruct(k_proj.shape, BF16),
        jax.ShapeDtypeStruct(v_proj.shape, BF16),
        jax.ShapeDtypeStruct((1, BLOCK), F32),
        jax.ShapeDtypeStruct((1, BLOCK), F32),
    )
    both = pltpu.VMEM((groups, BLOCK + HALF, 2 * BLOCK), BF16)
    out = pl.pallas_call(
        functools.partial(kernel, n, n_dp, groups, per_group),
        out_shape=shapes,
        in_specs=[hbm] * 11,
        out_specs=(hbm,) * 5,
        scratch_shapes=[
            pltpu.SMEM(dispatch_plan.shape, jnp.int32),
            pltpu.VMEM(k_proj.shape, BF16),
            pltpu.VMEM(v_proj.shape, BF16),
            pltpu.VMEM((1, BLOCK), F32),
            pltpu.VMEM((1, BLOCK), F32),
            pltpu.VMEM((3, 1, BLOCK), jnp.int32),
            pltpu.VMEM((1, count), jnp.int32),
            pltpu.VMEM((1, count), jnp.int32),
            pltpu.VMEM((1, count), jnp.int32),
            pltpu.VMEM(q_proj.shape, BF16),
            pltpu.VMEM(q_proj.shape, BF16),
            pltpu.VMEM((BLOCK, heads * BLOCK), BF16),
            pltpu.VMEM(k_proj.shape, BF16),
            pltpu.VMEM(v_proj.shape, BF16),
            pltpu.VMEM((2, 1, BLOCK), F32),
            pltpu.VMEM((groups, per_group * BLOCK, BLOCK), BF16),
            pltpu.VMEM((heads, BLOCK, 1), F32),
            pltpu.VMEM((groups, per_group * BLOCK, BLOCK), F32),
            whole,
            whole,
            half,
            whole,
            whole,
            half,
            pltpu.VMEM((groups, SPAN, 2 * BLOCK), F32),
            whole,
            half,
            both,
            both,
            half,
            whole,
            whole,
            whole,
            pltpu.VMEM((n, 8, BLOCK), F32),
            pltpu.VMEM((n_dp, 8, BLOCK), F32),
            dma((11,)),
            dma((groups + 4,)),
        ]
        + [dma((groups,))] * 18
        + [dma((n,))] * 2
        + [dma((n_dp,))] * 2,
        compiler_params=pltpu.CompilerParams(
            collective_id=0, has_side_effects=True, vmem_limit_bytes=VMEM_LIMIT
        ),
        cost_estimate=pl.CostEstimate(
            flops=10 * heads * BLOCK * SPAN * BLOCK,
            bytes_accessed=6 * BLOCK * heads * BLOCK,
            transcendentals=heads * BLOCK * SPAN,
        ),
    )(
        dispatch_plan,
        k_proj,
        v_proj,
        q_gain.reshape(1, BLOCK),
        k_gain.reshape(1, BLOCK),
        pos_ids.transpose(1, 0, 2),
        stretch_lengths,
        stretch_windows,
        clip_ids,
        q_proj,
        out_grad,
    )
    out = pl.pallas_call(
        hand_over,
        out_shape=shapes,
        in_specs=[hbm] * 5,
        out_specs=(hbm,) * 5,
        scratch_shapes=[pltpu.VMEM(shape.shape, shape.dtype) for shape in shapes]
        + [dma((8,))] * 2,
    )(*out)
    return (out[0], out[1], out[2], out[3].reshape(BLOCK), out[4].reshape(BLOCK))


def solution(mesh):
    row = P("dp", "ctx", None)
    table = P("dp", None)
    return jax.shard_map(
        shards,
        mesh=mesh,
        in_specs=(row, row, row, row, P(), P(), P("dp", None, "ctx"), table, table, table, table),
        out_specs=(row, row, row, P(), P()),
        check_vma=False,
    )
```

profile of v0, /device:TPU:0, one launch (start us, length us, event | category | flops | bytes accessed | tf_op | source)
XLA Modules:
  0.0 34.0 jit_solution(4549623904552874141)
XLA Ops:
  0.6 31.2 %shard_map.146 = (bf16[1,128,3072]{2,1,0:T(8,128)(2,1)}, bf16[1,128,512]{2,1,0:T(8,128)(2,1)}, bf16[1,128,512]{2,1,0:T(8,128)(2,1)}, f32[1,128]{1,0:T(1,128)}, f32[1,128]{1,0:T(1,128)}) custom-call(s32[1,8]{1,0:T(1,128)} %plan_hbm.1, bf16[1,128,512]{2,1,0:T(8,128)(2,1)} %k_hbm.1, bf16[1,128,512]{2,1,0:T(8,128)(2,1)} %v_hbm.1, f32[1,128]{1,0:T(1,128)} %bitcast.6, ...), custom_call_target="tpu_custom_call" | custom-call | flops 1258291200 | bytes 2359296 | tf_op jit(solution)/shard_map/pallas_call | solution.py:626
  31.9 2.1 %shard_map.147 = (bf16[1,128,3072]{2,1,0:T(8,128)(2,1)}, bf16[1,128,512]{2,1,0:T(8,128)(2,1)}, bf16[1,128,512]{2,1,0:T(8,128)(2,1)}, f32[1,128]{1,0:T(1,128)}, f32[1,128]{1,0:T(1,128)}) custom-call(bf16[1,128,3072]{2,1,0:T(8,128)(2,1)} %get-tuple-element.15.refs_0_, bf16[1,128,512]{2,1,0:T(8,128)(2,1)} %get-tuple-element.16.refs_1_, ...), custom_call_target="tpu_custom_call" | custom-call | tf_op jit(solution)/shard_map/pallas_call | solution.py:694
where the time goes:
time: 34.2 us; the launch traced here: 34 us
  Pallas kernels  33.3 us (97%)
  between operations  0.64 us (2%)
    pallas_call x1, Pallas kernels, shards(): pl.pallas_call(functools.partial(kernel, n, n_dp, groups, per_group), out...  31.2 us
    pallas_call x1, Pallas kernels, shards(): pl.pallas_call(hand_over, out_shape=shapes, in_specs=[hbm] * 5, out_specs...  2.13 us

commit v1 on v0

--- a/solution.py
+++ b/solution.py
@@ -15,7 +15,7 @@
 HALF = BLOCK // 2
 SPAN = 2 * BLOCK + HALF
 norm_eps = 1e-06
-VMEM_LIMIT = 60 * 1024 * 1024
+VMEM_LIMIT = 40 * 1024 * 1024
 rope_base = 10000.0
 
 NT = (((1,), (1,)), ((), ()))
@@ -104,11 +104,11 @@
     clip_hbm,
     q_hbm,
     do_hbm,
-    qgrad_hbm,
-    kgrad_hbm,
-    vgrad_hbm,
-    qgain_hbm,
-    kgain_hbm,
+    qgrad_ref,
+    kgrad_ref,
+    vgrad_ref,
+    qgain_ref,
+    kgain_ref,
     plan_ref,
     k_ref,
     v_ref,
@@ -120,10 +120,6 @@
     clip_ref,
     q_vm,
     do_vm,
-    qout,
-    kgrad_ref,
-    vgrad_ref,
-    gain_ref,
     qrot,
     qinv,
     dq,
@@ -145,7 +141,6 @@
     term_ctx,
     term_dp,
     load_sem,
-    out_sem,
     pair_s,
     pair_r,
     np_s,
@@ -174,7 +169,6 @@
     partner = me + 1 - 2 * lax.rem(me, 2)
     has_prev = me >= 2
     has_next = me < n - 2
-    width = per_group * BLOCK
     inv_sqrt = BLOCK ** (-0.5)
 
     sources = (
@@ -436,7 +430,6 @@
     send_back(order[-1])
     cos_back, sin_back = cosine * inv_sqrt, sine * inv_sqrt
     q_term = jnp.zeros((BLOCK, BLOCK), F32)
-    outs = []
     for g in range(groups):
         for j in range(per_group):
             h = g * per_group + j
@@ -447,14 +440,9 @@
             product = turned * unit
             q_term = q_term + product
             mean = jnp.mean(product * q_gain, axis=1, keepdims=True)
-            qout[:, h * BLOCK : (h + 1) * BLOCK] = (inv * (turned * q_gain - unit * mean)).astype(
+            qgrad_ref[0, :, h * BLOCK : (h + 1) * BLOCK] = (inv * (turned * q_gain - unit * mean)).astype(
                 BF16
             )
-        columns = pl.ds(g * width, width)
-        outs.append(
-            pltpu.make_async_copy(qout.at[:, columns], qgrad_hbm.at[0, :, columns], out_sem.at[g])
-        )
-        outs[g].start()
 
     home = [
         remote(back_pair.at[g], home_pair.at[g], hp_s.at[g], hp_r.at[g], (dp, partner))
@@ -498,10 +486,6 @@
         k_term = k_term + product
         mean = jnp.mean(product * k_gain, axis=1, keepdims=True)
         kgrad_ref[0, :, columns] = (inv * (turned * k_gain - unit * mean)).astype(BF16)
-    outs.append(pltpu.make_async_copy(kgrad_ref, kgrad_hbm, out_sem.at[groups]))
-    outs.append(pltpu.make_async_copy(vgrad_ref, vgrad_hbm, out_sem.at[groups + 1]))
-    outs[groups].start()
-    outs[groups + 1].start()
 
     term_ctx[me, 0:1] = jnp.sum(q_term, axis=0, keepdims=True)
     term_ctx[me, 1:2] = jnp.sum(k_term, axis=0, keepdims=True)
@@ -552,44 +536,19 @@
     lax.fori_loop(1, n_dp, run(dp_copy, "wait_recv"), 0)
     sums = jnp.sum(term_dp[:, 0:2], axis=0)
     token_count = n_dp * n * BLOCK
-    gain_ref[0] = sums[0:1] * (1.0 / math.sqrt(token_count * groups * per_group))
-    gain_ref[1] = sums[1:2] * (1.0 / math.sqrt(token_count * groups))
-    outs.append(pltpu.make_async_copy(gain_ref.at[0], qgain_hbm, out_sem.at[groups + 2]))
-    outs.append(pltpu.make_async_copy(gain_ref.at[1], kgain_hbm, out_sem.at[groups + 3]))
-    outs[groups + 2].start()
-    outs[groups + 3].start()
+    qgain_ref[...] = sums[0:1] * (1.0 / math.sqrt(token_count * groups * per_group))
+    kgain_ref[...] = sums[1:2] * (1.0 / math.sqrt(token_count * groups))
     lax.fori_loop(1, n_dp, run(dp_copy, "wait_send"), 0)
-    for out in outs:
-        out.wait()
 
 
 def hand_over(*refs):
-    count = (len(refs) - 2) // 3
-    sources, targets, middles = refs[:count], refs[count : 2 * count], refs[2 * count : -2]
-    arrive, leave = refs[-2:]
-    pieces = []
-    for source, target, middle in zip(sources, targets, middles):
-        if len(source.shape) == 3 and source.shape[2] >= 1024:
-            rows = source.shape[1] // 4
-            spots = [(0, slice(i * rows, (i + 1) * rows)) for i in range(4)]
-        else:
-            spots = [(slice(None),)]
-        pieces += [(source.at[spot], middle.at[spot], target.at[spot]) for spot in spots]
-    first = [
-        pltpu.make_async_copy(source, middle, arrive.at[i])
-        for i, (source, middle, target) in enumerate(pieces)
-    ]
-    second = [
-        pltpu.make_async_copy(middle, target, leave.at[i])
-        for i, (source, middle, target) in enumerate(pieces)
-    ]
-    for copy in first:
-        copy.start()
-    for copy, later in zip(first, second):
-        copy.wait()
-        later.start()
-    for later in second:
-        later.wait()
+    count = (len(refs) - 1) // 2
+    sems = refs[-1]
+    copies = [pltpu.make_async_copy(s, d, sems.at[i]) for i, (s, d) in enumerate(zip(refs[:count], refs[count:2*count]))]
+    for c in copies:
+        c.start()
+    for c in copies:
+        c.wait()
 
 
 def shards(
@@ -625,9 +584,9 @@
     both = pltpu.VMEM((groups, BLOCK + HALF, 2 * BLOCK), BF16)
     out = pl.pallas_call(
         functools.partial(kernel, n, n_dp, groups, per_group),
-        out_shape=shapes,
-        in_specs=[hbm] * 11,
-        out_specs=(hbm,) * 5,
+        out_shape=tuple(pltpu.VMEM(s.shape, s.dtype) for s in shapes),
+        in_specs=[pl.BlockSpec(memory_space=pltpu.HBM)] * 11,
+        out_specs=(pl.BlockSpec(memory_space=pltpu.VMEM),) * 5,
         scratch_shapes=[
             pltpu.SMEM(dispatch_plan.shape, jnp.int32),
             pltpu.VMEM(k_proj.shape, BF16),
@@ -640,10 +599,6 @@
             pltpu.VMEM((1, count), jnp.int32),
             pltpu.VMEM(q_proj.shape, BF16),
             pltpu.VMEM(q_proj.shape, BF16),
-            pltpu.VMEM((BLOCK, heads * BLOCK), BF16),
-            pltpu.VMEM(k_proj.shape, BF16),
-            pltpu.VMEM(v_proj.shape, BF16),
-            pltpu.VMEM((2, 1, BLOCK), F32),
             pltpu.VMEM((groups, per_group * BLOCK, BLOCK), BF16),
             pltpu.VMEM((heads, BLOCK, 1), F32),
             pltpu.VMEM((groups, per_group * BLOCK, BLOCK), F32),
@@ -665,7 +620,6 @@
             pltpu.VMEM((n, 8, BLOCK), F32),
             pltpu.VMEM((n_dp, 8, BLOCK), F32),
             dma((11,)),
-            dma((groups + 4,)),
         ]
         + [dma((groups,))] * 18
         + [dma((n,))] * 2
@@ -678,7 +632,7 @@
             bytes_accessed=6 * BLOCK * heads * BLOCK,
             transcendentals=heads * BLOCK * SPAN,
         ),
-    )(
+    )(*[pltpu.with_memory_space_constraint(a, pltpu.HBM) for a in (
         dispatch_plan,
         k_proj,
         v_proj,
@@ -690,15 +644,14 @@
         clip_ids,
         q_proj,
         out_grad,
-    )
+    )])
     out = pl.pallas_call(
         hand_over,
-        out_shape=shapes,
+        out_shape=tuple(pltpu.HBM(s.shape, s.dtype) for s in shapes),
         in_specs=[hbm] * 5,
-        out_specs=(hbm,) * 5,
-        scratch_shapes=[pltpu.VMEM(shape.shape, shape.dtype) for shape in shapes]
-        + [dma((8,))] * 2,
-    )(*out)
+        out_specs=(pl.BlockSpec(memory_space=pltpu.HBM),) * 5,
+        scratch_shapes=[dma((8,))],
+    )(*[pltpu.with_memory_space_constraint(o, pltpu.VMEM) for o in out])
     return (out[0], out[1], out[2], out[3].reshape(BLOCK), out[4].reshape(BLOCK))
 
 

time: 34.2 us -> 32.4 us (0.947)
  Pallas kernels: 33.3 us -> 31.6 us
    pallas_call x1, Pallas kernels: 2.13 us -> 1.03 us  [shards(): pl.pallas_call(hand_over, out_shape=tuple((pltpu.HBM(s.shape, s.dtype) fo...]
    pallas_call x1, Pallas kernels: 31.2 us -> 30.6 us  [shards(): pl.pallas_call(functools.partial(kernel, n, n_dp, groups, per_group), out...]
where the time goes in v1:
time: 32.4 us; the launch traced here: 32.3 us
  Pallas kernels  31.6 us (98%)
  between operations  0.64 us (2%)
    pallas_call x1, Pallas kernels, shards(): pl.pallas_call(functools.partial(kernel, n, n_dp, groups, per_group), out...  30.6 us
    pallas_call x1, Pallas kernels, shards(): pl.pallas_call(hand_over, out_shape=tuple((pltpu.HBM(s.shape, s.dtype) fo...  1.03 us

profile of v1, /device:TPU:0, one launch (start us, length us, event | category | flops | bytes accessed | tf_op | source)
XLA Modules:
  0.0 32.3 jit_solution(11763948755330870512)
XLA Ops:
  0.6 30.6 %shard_map.146 = (bf16[1,128,3072]{2,1,0:T(8,128)(2,1)S(1)}, bf16[1,128,512]{2,1,0:T(8,128)(2,1)S(1)}, bf16[1,128,512]{2,1,0:T(8,128)(2,1)S(1)}, f32[1,128]{1,0:T(1,128)S(1)}, f32[1,128]{1,0:T(1,128)S(1)}) custom-call(s32[1,8]{1,0:T(1,128)} %plan_hbm.1, bf16[1,128,512]{2,1,0:T(8,128)(2,1)} %k_hbm.1, bf16[1,128,512]{2,1,0:T(8,128)(2,1)} %v_hbm.1, ...), custom_call_target="tpu_custom_call" | custom-call | flops 1258291200 | bytes 2359296 | tf_op jit(solution)/shard_map/pallas_call | solution.py:585
  31.2 1.0 %shard_map.147 = (bf16[1,128,3072]{2,1,0:T(8,128)(2,1)}, bf16[1,128,512]{2,1,0:T(8,128)(2,1)}, bf16[1,128,512]{2,1,0:T(8,128)(2,1)}, f32[1,128]{1,0:T(1,128)}, f32[1,128]{1,0:T(1,128)}) custom-call(bf16[1,128,3072]{2,1,0:T(8,128)(2,1)S(1)} %get-tuple-element.15.refs_0_, bf16[1,128,512]{2,1,0:T(8,128)(2,1)S(1)} %get-tuple-element.16.refs_1_, ...), custom_call_target="tpu_custom_call" | custom-call | tf_op jit(solution)/shard_map/pallas_call | solution.py:648

commit v2 on v1

v2 whole, which is shorter than its diff:
```python
import functools
import math

import jax
import jax.numpy as jnp
from jax import lax
from jax.experimental import pallas as pl
from jax.experimental.pallas import tpu as pltpu
from jax.sharding import PartitionSpec as P

MESH = pl.DeviceIdType.MESH
F32 = jnp.float32
BF16 = jnp.bfloat16
BLOCK = 128
HALF = BLOCK // 2
SPAN = 2 * BLOCK + HALF
norm_eps = 1e-06
VMEM_LIMIT = 40 * 1024 * 1024
rope_base = 10000.0

NT = (((1,), (1,)), ((), ()))
TN = (((0,), (0,)), ((), ()))


def sin_cos(angle):
    turns = jnp.floor(angle * (2.0 / math.pi) + 0.5)
    rest = angle - turns * 1.5703125
    rest = rest - turns * 4.837512969970703125e-4
    rest = rest - turns * 7.549789948768648e-8
    square = rest * rest
    sine = rest + rest * square * (
        -1.6666654611e-1 + square * (8.3321608736e-3 + square * -1.9515295891e-4)
    )
    cosine = (
        1.0
        - 0.5 * square
        + square
        * square
        * (4.166664568298827e-2 + square * (-1.388731625493765e-3 + square * 2.443315711809948e-5))
    )
    quarter = turns.astype(jnp.int32)
    odd = (quarter & 1) == 1
    sine_out = jnp.where(odd, cosine, sine)
    cosine_out = jnp.where(odd, sine, cosine)
    sine_out = jnp.where((quarter & 2) == 2, -sine_out, sine_out)
    cosine_out = jnp.where(((quarter + 1) & 2) == 2, -cosine_out, cosine_out)
    return sine_out, cosine_out


def roll_half(x):
    return pltpu.roll(x, HALF, 1)


def rope_tables(ids):
    rows = lax.broadcasted_iota(jnp.int32, (BLOCK, BLOCK), 0)
    lanes = lax.broadcasted_iota(jnp.int32, (BLOCK, BLOCK), 1)
    columns = [
        jnp.sum(jnp.where(rows == lanes, ids[t].astype(F32), 0.0), axis=1, keepdims=True)
        for t in range(3)
    ]
    pair = lanes % HALF
    chosen = jnp.where(pair < 16, columns[0], jnp.where(pair < 40, columns[1], columns[2]))
    pair_row = lax.broadcasted_iota(jnp.int32, (1, BLOCK), 1) % HALF
    frequency = jnp.exp(pair_row.astype(F32) * (-math.log(rope_base) / HALF))
    sine, cosine = sin_cos(chosen * frequency)
    return cosine, jnp.where(lanes < HALF, -sine, sine)


def key_ranges(lengths, windows, clips, start):
    count = lengths.shape[1]
    rows = lax.broadcasted_iota(jnp.int32, (count, count), 0)
    lanes = lax.broadcasted_iota(jnp.int32, (count, count), 1)

    def column(where_, values):
        return jnp.sum(jnp.where(where_, values.astype(F32), 0.0), axis=1, keepdims=True)

    ends = column(lanes <= rows, lengths)
    starts = column(lanes < rows, lengths)
    before = column(lanes == rows - 1, lengths)
    window = column(lanes == rows, windows)
    clip = column(lanes == rows, clips + 1)
    clip_before = column(lanes == rows - 1, clips + 1)
    low = starts - jnp.where(clip == clip_before, window * before, 0.0)
    spots = (start + lax.broadcasted_iota(jnp.int32, (count, BLOCK), 1)).astype(F32)
    inside = (starts <= spots) & (spots < ends)
    low_row = jnp.sum(jnp.where(inside, low, 0.0), axis=0, keepdims=True)
    high_row = jnp.sum(jnp.where(inside, ends, 0.0), axis=0, keepdims=True)
    return low_row, high_row


def lane_sums(x, ones):
    high = x.astype(BF16)
    low = (x - high.astype(F32)).astype(BF16)
    return jnp.dot(jnp.concatenate([high, low], axis=1), ones, preferred_element_type=F32)


def fold_rows(x):
    return jnp.sum(x.reshape(x.shape[0] // 8, 8, x.shape[1]), axis=0)


def kernel(n, n_dp, groups, per_group, *refs):
    share = groups // 2
    wide = per_group * BLOCK
    refs = iter(refs)

    def take(count):
        return [next(refs) for _ in range(count)]

    (
        plan_hbm,
        k_hbm,
        v_hbm,
        qg_hbm,
        kg_hbm,
        ids_hbm,
        len_hbm,
        win_hbm,
        clip_hbm,
        q_hbm,
        do_hbm,
    ) = take(11)
    qgrad_ref, kgrad_ref, vgrad_ref, qgain_ref, kgain_ref = take(5)
    plan_ref, qg_ref, kg_ref, ids, near_ids, len_ref, win_ref, clip_ref = take(8)
    k_raw, v_raw, cosn, sinn, near_cos, near_sin, bias_ref, dk_all = take(8)
    k_out, v_out, term_pair, term_ctx, term_dp = take(5)
    q_in = take(share)
    do_in = take(share)
    kv = take(share)
    rolled = take(share)
    qrot = take(share)
    qinv = take(share)
    central = [take(2) for _ in range(share)]
    central_grad = [take(2) for _ in range(share)]
    probs_low = [take(2) for _ in range(share)]
    score_grad = [take(2) for _ in range(share)]
    dkv = take(share)
    dq = take(share)
    back_prev = take(share)
    back_next = take(share)
    arrived = take(share)
    q_out = take(share)
    load_sem, sent, got, near_s, near_r, tc_s, tc_r, td_s, td_r = take(9)

    me = lax.axis_index("ctx")
    dp = lax.axis_index("dp")
    core = lax.rem(me, 2)
    pair = me // 2
    partner = me + 1 - 2 * core
    has_prev = me >= 2
    has_next = me < n - 2
    inv_sqrt = BLOCK ** (-0.5)

    def columns(which, width, j=0):
        return pl.ds(pl.multiple_of(which * (share * width) + j * width, BLOCK), width)

    mine, theirs = core, 1 - core
    both_k = pl.ds(pl.multiple_of(mine * (share * BLOCK), BLOCK), share * BLOCK)
    their_k = pl.ds(pl.multiple_of(theirs * (share * BLOCK), BLOCK), share * BLOCK)
    moves = [
        (plan_hbm, plan_ref),
        (ids_hbm, ids.at[0]),
        (qg_hbm, qg_ref),
        (kg_hbm, kg_ref),
        (k_hbm.at[0, :, both_k], k_raw.at[0]),
        (v_hbm.at[0, :, both_k], v_raw.at[0]),
        (len_hbm, len_ref),
        (win_hbm, win_ref),
        (clip_hbm, clip_ref),
    ]
    for j in range(share):
        moves.append((q_hbm.at[0, :, columns(mine, wide, j)], q_in[j].at[0]))
        moves.append((do_hbm.at[0, :, columns(mine, wide, j)], do_in[j].at[0]))
    loads = [
        pltpu.make_async_copy(source, target, load_sem.at[i])
        for i, (source, target) in enumerate(moves)
    ]

    barrier = pltpu.get_barrier_semaphore()
    pl.semaphore_signal(barrier, inc=1, device_id=(dp, partner), device_id_type=MESH)

    def greet_ctx(step, carry):
        peer = lax.rem(partner + step, n)

        @pl.when(peer != me)
        def _():
            pl.semaphore_signal(barrier, inc=1, device_id=(dp, peer), device_id_type=MESH)

        return carry

    def greet_dp(step, carry):
        peer = lax.rem(dp + step, n_dp)
        pl.semaphore_signal(barrier, inc=1, device_id=(peer, me), device_id_type=MESH)
        return carry

    lax.fori_loop(1, n, greet_ctx, 0)
    lax.fori_loop(1, n_dp, greet_dp, 0)
    for load in loads:
        load.start()

    @pl.when(jnp.logical_not(has_prev))
    def _():
        near_ids[0] = jnp.zeros_like(near_ids[0])
        for j in range(share):
            kv[j][:BLOCK] = jnp.zeros((BLOCK, 2 * BLOCK), BF16)
            arrived[j][0, :HALF] = jnp.zeros((HALF, 2 * BLOCK), BF16)

    @pl.when(jnp.logical_not(has_next))
    def _():
        near_ids[1] = jnp.zeros_like(near_ids[1])
        for j in range(share):
            kv[j][3 * BLOCK :] = jnp.zeros((HALF, 2 * BLOCK), BF16)
            arrived[j][1] = jnp.zeros((BLOCK, 2 * BLOCK), BF16)

    for j in range(share):
        arrived[j][0, HALF:] = jnp.zeros((HALF, 2 * BLOCK), BF16)

    def remote(source, target, send, receive, peer):
        return pltpu.make_async_remote_copy(
            src_ref=source,
            dst_ref=target,
            send_sem=send,
            recv_sem=receive,
            device_id=peer,
            device_id_type=MESH,
        )

    count = [0]

    def numbered(source, target, peer):
        i = count[0]
        count[0] += 1
        return remote(source, target, sent.at[i], got.at[i], (dp, peer))

    k_swap = numbered(k_hbm.at[0, :, their_k], k_raw.at[1], partner)
    v_swap = numbered(v_hbm.at[0, :, their_k], v_raw.at[1], partner)
    ids_swap = numbered(ids_hbm, ids.at[1], partner)
    q_swap = [
        numbered(q_hbm.at[0, :, columns(theirs, wide, j)], q_in[j].at[1], partner)
        for j in range(share)
    ]
    do_swap = [
        numbered(do_hbm.at[0, :, columns(theirs, wide, j)], do_in[j].at[1], partner)
        for j in range(share)
    ]
    to_next = [
        numbered(kv[j].at[2 * BLOCK : 3 * BLOCK], kv[j].at[:BLOCK], me + 2) for j in range(share)
    ]
    to_prev = [
        numbered(kv[j].at[BLOCK : BLOCK + HALF], kv[j].at[3 * BLOCK :], me - 2)
        for j in range(share)
    ]
    home_prev = [numbered(back_prev[j], arrived[j].at[1], me - 2) for j in range(share)]
    home_next = [numbered(back_next[j], arrived[j].at[0, :HALF], me + 2) for j in range(share)]
    q_home = [
        numbered(q_out[j], qgrad_ref.at[mine, :, j * wide : (j + 1) * wide], partner)
        for j in range(share)
    ]
    k_home = numbered(k_out, kgrad_ref.at[mine], partner)
    v_home = numbered(v_out, vgrad_ref.at[mine], partner)
    term_swap = numbered(term_pair.at[0], term_pair.at[1], partner)

    def near_copy(side, other, sender):
        peer = 2 * pair + other + (2 if side == 0 else -2)
        return remote(
            ids_hbm,
            near_ids.at[side, sender],
            near_s.at[side, other],
            near_r.at[side, sender],
            (dp, peer),
        )

    pl.semaphore_wait(barrier, n - 1 + n_dp - 1)
    k_swap.start()
    v_swap.start()
    ids_swap.start()
    for j in range(share):
        q_swap[j].start()
        do_swap[j].start()

    @pl.when(has_next)
    def _():
        for other in range(2):
            near_copy(0, other, core).start()

    @pl.when(has_prev)
    def _():
        for other in range(2):
            near_copy(1, other, core).start()

    for load in loads[:9]:
        load.wait()
    odd = lax.rem(plan_ref[0, me], 2)
    slot_of = (odd, 1 - odd)
    q_gain, k_gain = qg_ref[...], kg_ref[...]
    ones = jnp.ones((2 * BLOCK, BLOCK), BF16)

    for t in range(2):
        start = (2 * pair + t) * BLOCK
        low_row, high_row = key_ranges(len_ref[...], win_ref[...], clip_ref[...], start)
        spots = (start - BLOCK + lax.broadcasted_iota(jnp.int32, (SPAN, BLOCK), 0)).astype(F32)
        bias_ref[t] = jnp.where((spots >= low_row) & (spots < high_row), 0.0, -1e30)

    ids_swap.wait_recv()
    for t in range(2):
        cosine, sine = rope_tables([ids[slot_of[t], i] for i in range(3)])
        cosn[t] = cosine
        sinn[t] = sine

    def table(t):
        return cosn[t], sinn[t]

    rolled_k_gain, rolled_q_gain = roll_half(k_gain), roll_half(q_gain)
    k_swap.wait_recv()
    v_swap.wait_recv()
    for j in range(share):
        lanes = slice(j * BLOCK, (j + 1) * BLOCK)
        for t in range(2):
            cosine, sine = table(t)
            x = k_raw[slot_of[t], :, lanes].astype(F32)
            inv = lax.rsqrt(lane_sums(x * x, ones) * (1.0 / BLOCK) + norm_eps)
            turned = inv * (x * (cosine * k_gain) + roll_half(x) * (sine * rolled_k_gain))
            spot = slice((1 + t) * BLOCK, (2 + t) * BLOCK)
            kv[j][spot, :BLOCK] = turned.astype(BF16)
            kv[j][spot, BLOCK:] = v_raw[slot_of[t], :, lanes]
            rolled[j][spot] = roll_half(turned).astype(BF16)

        @pl.when(has_next)
        def _():
            to_next[j].start()

        @pl.when(has_prev)
        def _():
            to_prev[j].start()

    def heads(value, m):
        return jnp.concatenate(
            [
                value[:, 2 * m * BLOCK : (2 * m + 1) * BLOCK],
                value[:, (2 * m + 1) * BLOCK : (2 * m + 2) * BLOCK],
            ],
            axis=0,
        )

    def stacked(value):
        return jnp.concatenate(
            [value[:, h * BLOCK : (h + 1) * BLOCK] for h in range(per_group)], axis=0
        )

    scale = inv_sqrt * math.log2(math.e)
    middle = (slice(BLOCK, SPAN), slice(0, 2 * BLOCK))
    edge = (slice(0, BLOCK), slice(2 * BLOCK, SPAN))
    offset = (0, BLOCK)

    def shifted(spot, t):
        return slice(spot.start + offset[t], spot.stop + offset[t])

    def scored(j, t, spot, m, cot):
        key = kv[j][shifted(spot, t), :BLOCK]
        value = kv[j][shifted(spot, t), BLOCK:]
        query = qrot[j][t, 2 * m * BLOCK : (2 * m + 2) * BLOCK, :]
        scores = lax.dot_general(key, query, NT, preferred_element_type=F32)
        grad = lax.dot_general(value, cot, NT, preferred_element_type=F32)
        bias = bias_ref[t, spot]
        weights = jnp.exp2(scores * scale + jnp.concatenate([bias, bias], axis=1))
        return weights, grad

    sums = {}
    for j in range(share):
        loads[9 + 2 * j].wait()
        loads[10 + 2 * j].wait()
        q_swap[j].wait_recv()
        do_swap[j].wait_recv()
        for t in range(2):
            cosine, sine = table(t)
            qc, qs = cosine * q_gain, sine * rolled_q_gain
            for h in range(per_group):
                lanes = slice(h * BLOCK, (h + 1) * BLOCK)
                x = q_in[j][slot_of[t], :, lanes].astype(F32)
                inv = lax.rsqrt(lane_sums(x * x, ones) * (1.0 / BLOCK) + norm_eps)
                qinv[j][t, :, lanes] = inv
                qrot[j][t, lanes, :] = (inv * (x * qc + roll_half(x) * qs)).astype(BF16)
            for m in range(per_group // 2):
                lanes = slice(2 * m * BLOCK, (2 * m + 2) * BLOCK)
                cot = heads(do_in[j][slot_of[t]], m)
                weights, grad = scored(j, t, middle[t], m, cot)
                central[j][t][:, lanes] = weights
                central_grad[j][t][:, lanes] = grad
                sums[j, t, m] = (
                    jnp.sum(weights, axis=0, keepdims=True),
                    jnp.sum(weights * grad, axis=0, keepdims=True),
                )

    @pl.when(has_prev)
    def _():
        for sender in range(2):
            near_copy(0, sender, sender).wait_recv()

    @pl.when(has_next)
    def _():
        for sender in range(2):
            near_copy(1, sender, sender).wait_recv()

    before = 1 - lax.rem(plan_ref[0, lax.max(2 * pair - 2, 0)], 2)
    after = lax.rem(plan_ref[0, lax.min(2 * pair + 2, n - 2)], 2)
    cosine, sine = rope_tables([near_ids[0, before, i] for i in range(3)])
    near_cos[:BLOCK] = cosine
    near_sin[:BLOCK] = sine
    cosine, sine = rope_tables([near_ids[1, after, i] for i in range(3)])
    near_cos[BLOCK:] = cosine[:HALF]
    near_sin[BLOCK:] = sine[:HALF]

    for j in range(share):

        @pl.when(has_prev)
        def _():
            to_next[j].wait_recv()

        @pl.when(has_next)
        def _():
            to_prev[j].wait_recv()

        for t in range(2):
            spot = edge[t]
            for m in range(per_group // 2):
                lanes = slice(2 * m * BLOCK, (2 * m + 2) * BLOCK)
                cot = heads(do_in[j][slot_of[t]], m)
                weights, grad = scored(j, t, spot, m, cot)
                total, delta = sums[j, t, m]
                inverse = 1.0 / (total + jnp.sum(weights, axis=0, keepdims=True))
                delta = (delta + jnp.sum(weights * grad, axis=0, keepdims=True)) * inverse
                sums[j, t, m] = (inverse, delta)
                probs = weights * inverse
                probs_low[j][t][spot, lanes] = probs.astype(BF16)
                score_grad[j][t][spot, lanes] = (probs * (grad - delta)).astype(BF16)
            key_grad = (
                jnp.dot(score_grad[j][t][spot], qrot[j][t], preferred_element_type=F32) * inv_sqrt
            )
            value_grad = jnp.dot(
                probs_low[j][t][spot],
                stacked(do_in[j][slot_of[t]]),
                preferred_element_type=F32,
            )
            dk_all[j, shifted(spot, t)] = key_grad
            back = (back_prev, back_next)[t][j]
            back[:, :BLOCK] = key_grad.astype(BF16)
            back[:, BLOCK:] = value_grad.astype(BF16)

            @pl.when((has_prev, has_next)[t])
            def _():
                (home_prev, home_next)[t][j].start()

    q_term = jnp.zeros((8, BLOCK), F32)
    k_term = jnp.zeros((8, BLOCK), F32)
    for j in range(share):
        own_key = kv[j][:, :BLOCK].astype(F32)
        rolled[j][:BLOCK] = roll_half(own_key[:BLOCK]).astype(BF16)
        rolled[j][3 * BLOCK :] = roll_half(own_key[3 * BLOCK :]).astype(BF16)
        parts = []
        for t in range(2):
            spot = middle[t]
            for m in range(per_group // 2):
                lanes = slice(2 * m * BLOCK, (2 * m + 2) * BLOCK)
                inverse, delta = sums[j, t, m]
                probs = central[j][t][:, lanes] * inverse
                probs_low[j][t][spot, lanes] = probs.astype(BF16)
                score_grad[j][t][spot, lanes] = (
                    probs * (central_grad[j][t][:, lanes] - delta)
                ).astype(BF16)
            key_grad = (
                jnp.dot(score_grad[j][t][spot], qrot[j][t], preferred_element_type=F32) * inv_sqrt
            )
            value_grad = jnp.dot(
                probs_low[j][t][spot],
                stacked(do_in[j][slot_of[t]]),
                preferred_element_type=F32,
            )
            parts.append((key_grad, value_grad))
            window = slice(offset[t], offset[t] + SPAN)
            keys = jnp.concatenate([kv[j][window, :BLOCK], rolled[j][window]], axis=1)
            dq[j][t] = lax.dot_general(score_grad[j][t][...], keys, TN, preferred_element_type=F32)
        for i in range(2):
            even, late = parts[0][i], parts[1][i]
            lanes = slice(i * BLOCK, (i + 1) * BLOCK)
            dkv[j][0, :, lanes] = even[:BLOCK] + late[:BLOCK]
            dkv[j][1, :HALF, lanes] = even[BLOCK:] + late[BLOCK : BLOCK + HALF]
            dkv[j][1, HALF:, lanes] = late[BLOCK + HALF :]
        for t in range(2):
            dk_all[j, (1 + t) * BLOCK : (2 + t) * BLOCK] = dkv[j][t, :, :BLOCK]
        key, grad = own_key, dk_all[j]
        cosine, sine = (
            jnp.concatenate([near[:BLOCK], own[0], own[1], near[BLOCK:]], axis=0)
            for near, own in ((near_cos, cosn), (near_sin, sinn))
        )
        product = (grad * cosine - roll_half(grad) * sine) * (
            key * cosine - rolled[j][...].astype(F32) * sine
        )
        k_term = k_term + fold_rows(product)

        for s in range(2):
            t = slot_of[s]
            cos_back, sin_back = cosn[t] * inv_sqrt, sinn[t] * inv_sqrt
            for h in range(per_group):
                lanes = slice(h * BLOCK, (h + 1) * BLOCK)
                grad = dq[j][t, lanes, :BLOCK]
                turned = grad * cos_back - dq[j][t, lanes, BLOCK:] * sin_back
                inv = qinv[j][t, :, lanes]
                unit = q_in[j][s, :, lanes].astype(F32) * inv
                product = turned * unit
                q_term = q_term + fold_rows(product)
                mean = lane_sums(product * q_gain, ones) * (1.0 / BLOCK)
                result = (inv * (turned * q_gain - unit * mean)).astype(BF16)
                if s == 0:
                    qgrad_ref[mine, :, j * wide + h * BLOCK : j * wide + (h + 1) * BLOCK] = result
                else:
                    q_out[j][:, lanes] = result
        q_home[j].start()

    term_pair[0, 0:1] = jnp.sum(q_term, axis=0, keepdims=True)
    term_pair[0, 1:2] = jnp.sum(k_term, axis=0, keepdims=True) / k_gain
    term_swap.start()

    def ctx_copy(step):
        peer = lax.rem(pair + step, n // 2)
        return remote(
            term_ctx.at[pair],
            term_ctx.at[pair],
            tc_s.at[step],
            tc_r.at[step],
            (dp, 2 * peer + core),
        )

    def dp_copy(step):
        peer = lax.rem(dp + step, n_dp)
        return remote(term_dp.at[dp], term_dp.at[dp], td_s.at[step], td_r.at[step], (peer, me))

    def run(copy_of, method):
        def body(step, carry):
            getattr(copy_of(step), method)()
            return carry

        return body

    term_swap.wait_recv()
    term_ctx[pair, 0:2] = term_pair[0, 0:2] + term_pair[1, 0:2]
    lax.fori_loop(1, n // 2, run(ctx_copy, "start"), 0)

    for j in range(share):

        @pl.when(has_next)
        def _():
            home_prev[j].wait_recv()

        @pl.when(has_prev)
        def _():
            home_next[j].wait_recv()

        lanes = slice(j * BLOCK, (j + 1) * BLOCK)
        for s in (1, 0):
            t = slot_of[s]
            cosine, sine = table(t)
            total = dkv[j][t] + arrived[j][t].astype(F32)
            grad = total[:, :BLOCK]
            x = k_raw[s, :, lanes].astype(F32)
            inv = lax.rsqrt(lane_sums(x * x, ones) * (1.0 / BLOCK) + norm_eps)
            unit = x * inv
            turned = grad * cosine - roll_half(grad) * sine
            mean = lane_sums(turned * unit * k_gain, ones) * (1.0 / BLOCK)
            result = (inv * (turned * k_gain - unit * mean)).astype(BF16)
            if s == 0:
                kgrad_ref[mine, :, lanes] = result
                vgrad_ref[mine, :, lanes] = total[:, BLOCK:].astype(BF16)
            else:
                k_out[:, lanes] = result
                v_out[:, lanes] = total[:, BLOCK:].astype(BF16)
    k_home.start()
    v_home.start()

    lax.fori_loop(1, n // 2, run(ctx_copy, "wait_recv"), 0)
    term_dp[dp, 0:2] = jnp.sum(term_ctx[:, 0:2], axis=0)
    lax.fori_loop(1, n_dp, run(dp_copy, "start"), 0)

    ids_swap.wait_send()
    k_swap.wait_send()
    v_swap.wait_send()
    for j in range(share):
        q_swap[j].wait_send()
        do_swap[j].wait_send()
        q_home[j].wait_recv()
        q_home[j].wait_send()

        @pl.when(has_next)
        def _():
            to_next[j].wait_send()
            home_next[j].wait_send()

        @pl.when(has_prev)
        def _():
            to_prev[j].wait_send()
            home_prev[j].wait_send()

    @pl.when(has_next)
    def _():
        for other in range(2):
            near_copy(0, other, core).wait_send()

    @pl.when(has_prev)
    def _():
        for other in range(2):
            near_copy(1, other, core).wait_send()

    term_swap.wait_send()
    lax.fori_loop(1, n // 2, run(ctx_copy, "wait_send"), 0)
    k_home.wait_recv()
    v_home.wait_recv()
    k_home.wait_send()
    v_home.wait_send()
    lax.fori_loop(1, n_dp, run(dp_copy, "wait_recv"), 0)
    totals = jnp.sum(term_dp[:, 0:2], axis=0)
    token_count = n_dp * n * BLOCK
    qgain_ref[...] = totals[0:1] * (1.0 / math.sqrt(token_count * groups * per_group))
    kgain_ref[...] = totals[1:2] * (1.0 / math.sqrt(token_count * groups))
    lax.fori_loop(1, n_dp, run(dp_copy, "wait_send"), 0)


def hand_over(*refs):
    sources, targets, sems = refs[:5], refs[5:10], refs[10]
    copies = []
    for source, target in zip(sources, targets):
        if len(source.shape) == 2:
            copies.append((source, target))
        else:
            width = source.shape[2]
            for half in range(2):
                lanes = slice(half * width, (half + 1) * width)
                copies.append((source.at[half], target.at[0, :, lanes]))
    copies = [
        pltpu.make_async_copy(source, target, sems.at[i])
        for i, (source, target) in enumerate(copies)
    ]
    for copy in copies:
        copy.start()
    for copy in copies:
        copy.wait()


def shards(
    q_proj,
    k_proj,
    v_proj,
    out_grad,
    q_gain,
    k_gain,
    pos_ids,
    stretch_lengths,
    stretch_windows,
    clip_ids,
    dispatch_plan,
):
    n = lax.axis_size("ctx")
    n_dp = lax.axis_size("dp")
    groups = k_proj.shape[2] // BLOCK
    heads = q_proj.shape[2] // BLOCK
    per_group = heads // groups
    share = groups // 2
    wide = per_group * BLOCK
    hbm = pl.BlockSpec(memory_space=pl.ANY)
    vmem = pl.BlockSpec(memory_space=pltpu.VMEM)
    dma = pltpu.SemaphoreType.DMA
    count = stretch_lengths.shape[1]
    nat = 3 * BLOCK + HALF
    central = (SPAN - BLOCK, 2 * BLOCK)
    out = pl.pallas_call(
        functools.partial(kernel, n, n_dp, groups, per_group),
        out_shape=(
            pltpu.VMEM((2, BLOCK, share * wide), BF16),
            pltpu.VMEM((2, BLOCK, share * BLOCK), BF16),
            pltpu.VMEM((2, BLOCK, share * BLOCK), BF16),
            pltpu.VMEM((1, BLOCK), F32),
            pltpu.VMEM((1, BLOCK), F32),
        ),
        in_specs=[hbm] * 11,
        out_specs=(vmem,) * 5,
        scratch_shapes=[
            pltpu.SMEM(dispatch_plan.shape, jnp.int32),
            pltpu.VMEM((1, BLOCK), F32),
            pltpu.VMEM((1, BLOCK), F32),
            pltpu.VMEM((2, 3, 1, BLOCK), jnp.int32),
            pltpu.VMEM((2, 2, 3, 1, BLOCK), jnp.int32),
            pltpu.VMEM((1, count), jnp.int32),
            pltpu.VMEM((1, count), jnp.int32),
            pltpu.VMEM((1, count), jnp.int32),
            pltpu.VMEM((2, BLOCK, share * BLOCK), BF16),
            pltpu.VMEM((2, BLOCK, share * BLOCK), BF16),
            pltpu.VMEM((2, BLOCK, BLOCK), F32),
            pltpu.VMEM((2, BLOCK, BLOCK), F32),
            pltpu.VMEM((BLOCK + HALF, BLOCK), F32),
            pltpu.VMEM((BLOCK + HALF, BLOCK), F32),
            pltpu.VMEM((2, SPAN, BLOCK), F32),
            pltpu.VMEM((share, nat, BLOCK), F32),
            pltpu.VMEM((BLOCK, share * BLOCK), BF16),
            pltpu.VMEM((BLOCK, share * BLOCK), BF16),
            pltpu.VMEM((2, 8, BLOCK), F32),
            pltpu.VMEM((n // 2, 8, BLOCK), F32),
            pltpu.VMEM((n_dp, 8, BLOCK), F32),
        ]
        + [pltpu.VMEM((2, BLOCK, wide), BF16)] * (2 * share)
        + [pltpu.VMEM((nat, 2 * BLOCK), BF16)] * share
        + [pltpu.VMEM((nat, BLOCK), BF16)] * share
        + [pltpu.VMEM((2, wide, BLOCK), BF16)] * share
        + [pltpu.VMEM((2, BLOCK, wide), F32)] * share
        + [pltpu.VMEM((rows, wide), F32) for rows in central] * (2 * share)
        + [pltpu.VMEM((SPAN, wide), BF16)] * (4 * share)
        + [pltpu.VMEM((2, BLOCK, 2 * BLOCK), F32)] * share
        + [pltpu.VMEM((2, wide, 2 * BLOCK), F32)] * share
        + [pltpu.VMEM((BLOCK, 2 * BLOCK), BF16)] * share
        + [pltpu.VMEM((HALF, 2 * BLOCK), BF16)] * share
        + [pltpu.VMEM((2, BLOCK, 2 * BLOCK), BF16)] * share
        + [pltpu.VMEM((BLOCK, wide), BF16)] * share
        + [
            dma((9 + 2 * share,)),
            dma((6 + 7 * share,)),
            dma((6 + 7 * share,)),
            dma((2, 2)),
            dma((2, 2)),
            dma((n // 2,)),
            dma((n // 2,)),
            dma((n_dp,)),
            dma((n_dp,)),
        ],
        compiler_params=pltpu.CompilerParams(
            collective_id=0, has_side_effects=True, vmem_limit_bytes=VMEM_LIMIT
        ),
        cost_estimate=pl.CostEstimate(
            flops=10 * heads * BLOCK * SPAN * BLOCK,
            bytes_accessed=6 * BLOCK * heads * BLOCK,
            transcendentals=heads * BLOCK * SPAN,
        ),
    )(
        *[
            pltpu.with_memory_space_constraint(array, pltpu.HBM)
            for array in (
                dispatch_plan,
                k_proj,
                v_proj,
                q_gain.reshape(1, BLOCK),
                k_gain.reshape(1, BLOCK),
                pos_ids.transpose(1, 0, 2),
                stretch_lengths,
                stretch_windows,
                clip_ids,
                q_proj,
                out_grad,
            )
        ]
    )
    out = pl.pallas_call(
        hand_over,
        out_shape=(
            pltpu.HBM(q_proj.shape, BF16),
            pltpu.HBM(k_proj.shape, BF16),
            pltpu.HBM(v_proj.shape, BF16),
            pltpu.HBM((1, BLOCK), F32),
            pltpu.HBM((1, BLOCK), F32),
        ),
        in_specs=[hbm] * 5,
        out_specs=(pl.BlockSpec(memory_space=pltpu.HBM),) * 5,
        scratch_shapes=[dma((8,))],
    )(*[pltpu.with_memory_space_constraint(array, pltpu.VMEM) for array in out])
    return (out[0], out[1], out[2], out[3].reshape(BLOCK), out[4].reshape(BLOCK))


def solution(mesh):
    row = P("dp", "ctx", None)
    table = P("dp", None)
    return jax.shard_map(
        shards,
        mesh=mesh,
        in_specs=(row, row, row, row, P(), P(), P("dp", None, "ctx"), table, table, table, table),
        out_specs=(row, row, row, P(), P()),
        check_vma=False,
    )
```

time: 32.4 us -> 28.3 us (0.87)
  Pallas kernels: 31.6 us -> 27.5 us
    pallas_call x1, Pallas kernels: 30.6 us -> 26.5 us  [shards(): pl.pallas_call(functools.partial(kernel, n, n_dp, groups, per_group), out...]
where the time goes in v2:
time: 28.3 us; the launch traced here: 28.1 us
  Pallas kernels  27.5 us (97%)
  between operations  0.64 us (2%)
    pallas_call x1, Pallas kernels, shards(): pl.pallas_call(functools.partial(kernel, n, n_dp, groups, per_group), out...  26.5 us
    pallas_call x1, Pallas kernels, shards(): pl.pallas_call(hand_over, out_shape=(pltpu.HBM(q_proj.shape, BF16), pltpu...  1.03 us

profile of v2, /device:TPU:0, one launch (start us, length us, event | category | flops | bytes accessed | tf_op | source)
XLA Modules:
  0.0 28.1 jit_solution(232438255511806799)
XLA Ops:
  0.6 26.5 %shard_map.146 = (bf16[2,128,1536]{2,1,0:T(8,128)(2,1)S(1)}, bf16[2,128,256]{2,1,0:T(8,128)(2,1)S(1)}, bf16[2,128,256]{2,1,0:T(8,128)(2,1)S(1)}, f32[1,128]{1,0:T(1,128)S(1)}, f32[1,128]{1,0:T(1,128)S(1)}) custom-call(s32[1,8]{1,0:T(1,128)} %refs_0_.1, bf16[1,128,512]{2,1,0:T(8,128)(2,1)} %refs_1_.1, bf16[1,128,512]{2,1,0:T(8,128)(2,1)} %refs_2_.1, ...), custom_call_target="tpu_custom_call" | custom-call | flops 1258291200 | bytes 2359296 | tf_op jit(solution)/shard_map/pallas_call | solution.py:672
  27.1 1.0 %shard_map.147 = (bf16[1,128,3072]{2,1,0:T(8,128)(2,1)}, bf16[1,128,512]{2,1,0:T(8,128)(2,1)}, bf16[1,128,512]{2,1,0:T(8,128)(2,1)}, f32[1,128]{1,0:T(1,128)}, f32[1,128]{1,0:T(1,128)}) custom-call(bf16[2,128,1536]{2,1,0:T(8,128)(2,1)S(1)} %get-tuple-element.15.refs_0_, bf16[2,128,256]{2,1,0:T(8,128)(2,1)S(1)} %get-tuple-element.16.refs_1_, ...), custom_call_target="tpu_custom_call" | custom-call | tf_op jit(solution)/shard_map/pallas_call | solution.py:756

commit v3 on v2

--- a/solution.py
+++ b/solution.py
@@ -122,7 +122,7 @@
     qgrad_ref, kgrad_ref, vgrad_ref, qgain_ref, kgain_ref = take(5)
     plan_ref, qg_ref, kg_ref, ids, near_ids, len_ref, win_ref, clip_ref = take(8)
     k_raw, v_raw, cosn, sinn, near_cos, near_sin, bias_ref, dk_all = take(8)
-    k_out, v_out, term_pair, term_ctx, term_dp = take(5)
+    k_out, v_out, term_ctx, term_dp = take(4)
     q_in = take(share)
     do_in = take(share)
     kv = take(share)
@@ -139,6 +139,8 @@
     back_next = take(share)
     arrived = take(share)
     q_out = take(share)
+    q_turned = take(share)
+    q_unit = take(share)
     load_sem, sent, got, near_s, near_r, tc_s, tc_r, td_s, td_r = take(9)
 
     me = lax.axis_index("ctx")
@@ -257,7 +259,6 @@
     ]
     k_home = numbered(k_out, kgrad_ref.at[mine], partner)
     v_home = numbered(v_out, vgrad_ref.at[mine], partner)
-    term_swap = numbered(term_pair.at[0], term_pair.at[1], partner)
 
     def near_copy(side, other, sender):
         peer = 2 * pair + other + (2 if side == 0 else -2)
@@ -270,9 +271,9 @@
         )
 
     pl.semaphore_wait(barrier, n - 1 + n_dp - 1)
+    ids_swap.start()
     k_swap.start()
     v_swap.start()
-    ids_swap.start()
     for j in range(share):
         q_swap[j].start()
         do_swap[j].start()
@@ -294,20 +295,15 @@
     q_gain, k_gain = qg_ref[...], kg_ref[...]
     ones = jnp.ones((2 * BLOCK, BLOCK), BF16)
 
-    for t in range(2):
-        start = (2 * pair + t) * BLOCK
-        low_row, high_row = key_ranges(len_ref[...], win_ref[...], clip_ref[...], start)
-        spots = (start - BLOCK + lax.broadcasted_iota(jnp.int32, (SPAN, BLOCK), 0)).astype(F32)
-        bias_ref[t] = jnp.where((spots >= low_row) & (spots < high_row), 0.0, -1e30)
-
-    ids_swap.wait_recv()
-    for t in range(2):
-        cosine, sine = rope_tables([ids[slot_of[t], i] for i in range(3)])
-        cosn[t] = cosine
-        sinn[t] = sine
+    for s in range(2):
+        if s == 1:
+            ids_swap.wait_recv()
+        cosine, sine = rope_tables([ids[s, i] for i in range(3)])
+        cosn[s] = cosine
+        sinn[s] = sine
 
     def table(t):
-        return cosn[t], sinn[t]
+        return cosn[slot_of[t]], sinn[slot_of[t]]
 
     rolled_k_gain, rolled_q_gain = roll_half(k_gain), roll_half(q_gain)
     k_swap.wait_recv()
@@ -324,13 +320,19 @@
             kv[j][spot, BLOCK:] = v_raw[slot_of[t], :, lanes]
             rolled[j][spot] = roll_half(turned).astype(BF16)
 
+        @pl.when(has_prev)
+        def _():
+            to_prev[j].start()
+
         @pl.when(has_next)
         def _():
             to_next[j].start()
 
-        @pl.when(has_prev)
-        def _():
-            to_prev[j].start()
+    for t in range(2):
+        start = (2 * pair + t) * BLOCK
+        low_row, high_row = key_ranges(len_ref[...], win_ref[...], clip_ref[...], start)
+        spots = (start - BLOCK + lax.broadcasted_iota(jnp.int32, (SPAN, BLOCK), 0)).astype(F32)
+        bias_ref[t] = jnp.where((spots >= low_row) & (spots < high_row), 0.0, -1e30)
 
     def heads(value, m):
         return jnp.concatenate(
@@ -409,6 +411,15 @@
     near_cos[BLOCK:] = cosine[:HALF]
     near_sin[BLOCK:] = sine[:HALF]
 
+    def join(j, i, parts):
+        even, late = parts
+        lanes = slice(i * BLOCK, (i + 1) * BLOCK)
+        dkv[j][0, :, lanes] = even[:BLOCK] + late[:BLOCK]
+        dkv[j][1, :HALF, lanes] = even[BLOCK:] + late[BLOCK : BLOCK + HALF]
+        dkv[j][1, HALF:, lanes] = late[BLOCK + HALF :]
+
+    q_term = jnp.zeros((8, BLOCK), F32)
+    k_term = jnp.zeros((8, BLOCK), F32)
     for j in range(share):
 
         @pl.when(has_prev)
@@ -449,9 +460,6 @@
             def _():
                 (home_prev, home_next)[t][j].start()
 
-    q_term = jnp.zeros((8, BLOCK), F32)
-    k_term = jnp.zeros((8, BLOCK), F32)
-    for j in range(share):
         own_key = kv[j][:, :BLOCK].astype(F32)
         rolled[j][:BLOCK] = roll_half(own_key[:BLOCK]).astype(BF16)
         rolled[j][3 * BLOCK :] = roll_half(own_key[3 * BLOCK :]).astype(BF16)
@@ -466,29 +474,18 @@
                 score_grad[j][t][spot, lanes] = (
                     probs * (central_grad[j][t][:, lanes] - delta)
                 ).astype(BF16)
-            key_grad = (
+            parts.append(
                 jnp.dot(score_grad[j][t][spot], qrot[j][t], preferred_element_type=F32) * inv_sqrt
             )
-            value_grad = jnp.dot(
-                probs_low[j][t][spot],
-                stacked(do_in[j][slot_of[t]]),
-                preferred_element_type=F32,
-            )
-            parts.append((key_grad, value_grad))
             window = slice(offset[t], offset[t] + SPAN)
             keys = jnp.concatenate([kv[j][window, :BLOCK], rolled[j][window]], axis=1)
             dq[j][t] = lax.dot_general(score_grad[j][t][...], keys, TN, preferred_element_type=F32)
-        for i in range(2):
-            even, late = parts[0][i], parts[1][i]
-            lanes = slice(i * BLOCK, (i + 1) * BLOCK)
-            dkv[j][0, :, lanes] = even[:BLOCK] + late[:BLOCK]
-            dkv[j][1, :HALF, lanes] = even[BLOCK:] + late[BLOCK : BLOCK + HALF]
-            dkv[j][1, HALF:, lanes] = late[BLOCK + HALF :]
+        join(j, 0, parts)
         for t in range(2):
             dk_all[j, (1 + t) * BLOCK : (2 + t) * BLOCK] = dkv[j][t, :, :BLOCK]
         key, grad = own_key, dk_all[j]
         cosine, sine = (
-            jnp.concatenate([near[:BLOCK], own[0], own[1], near[BLOCK:]], axis=0)
+            jnp.concatenate([near[:BLOCK], own[odd], own[1 - odd], near[BLOCK:]], axis=0)
             for near, own in ((near_cos, cosn), (near_sin, sinn))
         )
         product = (grad * cosine - roll_half(grad) * sine) * (
@@ -496,53 +493,66 @@
         )
         k_term = k_term + fold_rows(product)
 
+    for j in range(share):
         for s in range(2):
             t = slot_of[s]
-            cos_back, sin_back = cosn[t] * inv_sqrt, sinn[t] * inv_sqrt
+            cos_back, sin_back = cosn[s] * inv_sqrt, sinn[s] * inv_sqrt
             for h in range(per_group):
                 lanes = slice(h * BLOCK, (h + 1) * BLOCK)
                 grad = dq[j][t, lanes, :BLOCK]
                 turned = grad * cos_back - dq[j][t, lanes, BLOCK:] * sin_back
-                inv = qinv[j][t, :, lanes]
-                unit = q_in[j][s, :, lanes].astype(F32) * inv
+                unit = q_in[j][s, :, lanes].astype(F32) * qinv[j][t, :, lanes]
                 product = turned * unit
                 q_term = q_term + fold_rows(product)
-                mean = lane_sums(product * q_gain, ones) * (1.0 / BLOCK)
-                result = (inv * (turned * q_gain - unit * mean)).astype(BF16)
+                q_turned[j][s, :, lanes] = turned
+                q_unit[j][s, :, lanes] = unit
+
+    term_dp[dp, 0:1] = jnp.sum(q_term, axis=0, keepdims=True)
+    term_dp[dp, 1:2] = jnp.sum(k_term, axis=0, keepdims=True) / k_gain
+
+    def ctx_copy(step):
+        peer = lax.rem(me + step, n)
+        return remote(term_ctx.at[me], term_ctx.at[me], tc_s.at[step], tc_r.at[step], (dp, peer))
+
+    def dp_copy(step):
+        peer = lax.rem(dp + step, n_dp)
+        return remote(term_dp.at[dp], term_dp.at[dp], td_s.at[step], td_r.at[step], (peer, me))
+
+    ctx_copies = [ctx_copy(step) for step in range(1, n)]
+    dp_copies = [dp_copy(step) for step in range(1, n_dp)]
+    for copy in dp_copies:
+        copy.start()
+
+    for j in range(share):
+        for s in (1, 0):
+            for h in range(per_group):
+                lanes = slice(h * BLOCK, (h + 1) * BLOCK)
+                turned, unit = q_turned[j][s, :, lanes], q_unit[j][s, :, lanes]
+                weighted = turned * q_gain
+                mean = lane_sums(weighted * unit, ones) * (1.0 / BLOCK)
+                result = (qinv[j][slot_of[s], :, lanes] * (weighted - unit * mean)).astype(BF16)
                 if s == 0:
                     qgrad_ref[mine, :, j * wide + h * BLOCK : j * wide + (h + 1) * BLOCK] = result
                 else:
                     q_out[j][:, lanes] = result
-        q_home[j].start()
-
-    term_pair[0, 0:1] = jnp.sum(q_term, axis=0, keepdims=True)
-    term_pair[0, 1:2] = jnp.sum(k_term, axis=0, keepdims=True) / k_gain
-    term_swap.start()
-
-    def ctx_copy(step):
-        peer = lax.rem(pair + step, n // 2)
-        return remote(
-            term_ctx.at[pair],
-            term_ctx.at[pair],
-            tc_s.at[step],
-            tc_r.at[step],
-            (dp, 2 * peer + core),
-        )
-
-    def dp_copy(step):
-        peer = lax.rem(dp + step, n_dp)
-        return remote(term_dp.at[dp], term_dp.at[dp], td_s.at[step], td_r.at[step], (peer, me))
-
-    def run(copy_of, method):
-        def body(step, carry):
-            getattr(copy_of(step), method)()
-            return carry
-
-        return body
-
-    term_swap.wait_recv()
-    term_ctx[pair, 0:2] = term_pair[0, 0:2] + term_pair[1, 0:2]
-    lax.fori_loop(1, n // 2, run(ctx_copy, "start"), 0)
+            if s == 1:
+                q_home[j].start()
+    for j in range(share):
+        parts = [
+            jnp.dot(
+                probs_low[j][t][middle[t]],
+                stacked(do_in[j][slot_of[t]]),
+                preferred_element_type=F32,
+            )
+            for t in range(2)
+        ]
+        join(j, 1, parts)
+
+    for copy in dp_copies:
+        copy.wait_recv()
+    term_ctx[me, 0:2] = jnp.sum(term_dp[:, 0:2], axis=0)
+    for copy in ctx_copies:
+        copy.start()
 
     for j in range(share):
 
@@ -557,7 +567,7 @@
         lanes = slice(j * BLOCK, (j + 1) * BLOCK)
         for s in (1, 0):
             t = slot_of[s]
-            cosine, sine = table(t)
+            cosine, sine = cosn[s], sinn[s]
             total = dkv[j][t] + arrived[j][t].astype(F32)
             grad = total[:, :BLOCK]
             x = k_raw[s, :, lanes].astype(F32)
@@ -575,10 +585,6 @@
     k_home.start()
     v_home.start()
 
-    lax.fori_loop(1, n // 2, run(ctx_copy, "wait_recv"), 0)
-    term_dp[dp, 0:2] = jnp.sum(term_ctx[:, 0:2], axis=0)
-    lax.fori_loop(1, n_dp, run(dp_copy, "start"), 0)
-
     ids_swap.wait_send()
     k_swap.wait_send()
     v_swap.wait_send()
@@ -608,18 +614,20 @@
         for other in range(2):
             near_copy(1, other, core).wait_send()
 
-    term_swap.wait_send()
-    lax.fori_loop(1, n // 2, run(ctx_copy, "wait_send"), 0)
+    for copy in dp_copies:
+        copy.wait_send()
     k_home.wait_recv()
     v_home.wait_recv()
     k_home.wait_send()
     v_home.wait_send()
-    lax.fori_loop(1, n_dp, run(dp_copy, "wait_recv"), 0)
-    totals = jnp.sum(term_dp[:, 0:2], axis=0)
+    for copy in ctx_copies:
+        copy.wait_recv()
+    totals = jnp.sum(term_ctx[:, 0:2], axis=0)
     token_count = n_dp * n * BLOCK
     qgain_ref[...] = totals[0:1] * (1.0 / math.sqrt(token_count * groups * per_group))
     kgain_ref[...] = totals[1:2] * (1.0 / math.sqrt(token_count * groups))
-    lax.fori_loop(1, n_dp, run(dp_copy, "wait_send"), 0)
+    for copy in ctx_copies:
+        copy.wait_send()
 
 
 def hand_over(*refs):
@@ -699,8 +707,7 @@
             pltpu.VMEM((share, nat, BLOCK), F32),
             pltpu.VMEM((BLOCK, share * BLOCK), BF16),
             pltpu.VMEM((BLOCK, share * BLOCK), BF16),
-            pltpu.VMEM((2, 8, BLOCK), F32),
-            pltpu.VMEM((n // 2, 8, BLOCK), F32),
+            pltpu.VMEM((n, 8, BLOCK), F32),
             pltpu.VMEM((n_dp, 8, BLOCK), F32),
         ]
         + [pltpu.VMEM((2, BLOCK, wide), BF16)] * (2 * share)
@@ -716,14 +723,15 @@
         + [pltpu.VMEM((HALF, 2 * BLOCK), BF16)] * share
         + [pltpu.VMEM((2, BLOCK, 2 * BLOCK), BF16)] * share
         + [pltpu.VMEM((BLOCK, wide), BF16)] * share
+        + [pltpu.VMEM((2, BLOCK, wide), F32)] * (2 * share)
         + [
             dma((9 + 2 * share,)),
-            dma((6 + 7 * share,)),
-            dma((6 + 7 * share,)),
+            dma((5 + 7 * share,)),
+            dma((5 + 7 * share,)),
             dma((2, 2)),
             dma((2, 2)),
-            dma((n // 2,)),
-            dma((n // 2,)),
+            dma((n,)),
+            dma((n,)),
             dma((n_dp,)),
             dma((n_dp,)),
         ],

time: 28.3 us -> 25 us (0.88)
  Pallas kernels: 27.5 us -> 24.3 us
    pallas_call x1, Pallas kernels: 26.5 us -> 23.2 us  [shards(): pl.pallas_call(functools.partial(kernel, n, n_dp, groups, per_group), out...]
where the time goes in v3:
time: 25 us; the launch traced here: 24.9 us
  Pallas kernels  24.3 us (97%)
  between operations  0.64 us (3%)
    pallas_call x1, Pallas kernels, shards(): pl.pallas_call(functools.partial(kernel, n, n_dp, groups, per_group), out...  23.2 us
    pallas_call x1, Pallas kernels, shards(): pl.pallas_call(hand_over, out_shape=(pltpu.HBM(q_proj.shape, BF16), pltpu...  1.03 us

profile of v3, /device:TPU:0, one launch (start us, length us, event | category | flops | bytes accessed | tf_op | source)
XLA Modules:
  0.0 24.9 jit_solution(12340828124143992557)
XLA Ops:
  0.6 23.2 %shard_map.146 = (bf16[2,128,1536]{2,1,0:T(8,128)(2,1)S(1)}, bf16[2,128,256]{2,1,0:T(8,128)(2,1)S(1)}, bf16[2,128,256]{2,1,0:T(8,128)(2,1)S(1)}, f32[1,128]{1,0:T(1,128)S(1)}, f32[1,128]{1,0:T(1,128)S(1)}) custom-call(s32[1,8]{1,0:T(1,128)} %refs_0_.1, bf16[1,128,512]{2,1,0:T(8,128)(2,1)} %refs_1_.1, bf16[1,128,512]{2,1,0:T(8,128)(2,1)} %refs_2_.1, ...), custom_call_target="tpu_custom_call" | custom-call | flops 1258291200 | bytes 2359296 | tf_op jit(solution)/shard_map/pallas_call | solution.py:680
  23.9 1.0 %shard_map.147 = (bf16[1,128,3072]{2,1,0:T(8,128)(2,1)}, bf16[1,128,512]{2,1,0:T(8,128)(2,1)}, bf16[1,128,512]{2,1,0:T(8,128)(2,1)}, f32[1,128]{1,0:T(1,128)}, f32[1,128]{1,0:T(1,128)}) custom-call(bf16[2,128,1536]{2,1,0:T(8,128)(2,1)S(1)} %get-tuple-element.15.refs_0_, bf16[2,128,256]{2,1,0:T(8,128)(2,1)S(1)} %get-tuple-element.16.refs_1_, ...), custom_call_target="tpu_custom_call" | custom-call | tf_op jit(solution)/shard_map/pallas_call | solution.py:764

commit v4 on v3

--- a/solution.py
+++ b/solution.py
@@ -192,6 +192,7 @@
     def greet_dp(step, carry):
         peer = lax.rem(dp + step, n_dp)
         pl.semaphore_signal(barrier, inc=1, device_id=(peer, me), device_id_type=MESH)
+        pl.semaphore_signal(barrier, inc=1, device_id=(peer, partner), device_id_type=MESH)
         return carry
 
     lax.fori_loop(1, n, greet_ctx, 0)
@@ -270,7 +271,7 @@
             (dp, peer),
         )
 
-    pl.semaphore_wait(barrier, n - 1 + n_dp - 1)
+    pl.semaphore_wait(barrier, n - 1 + 2 * (n_dp - 1))
     ids_swap.start()
     k_swap.start()
     v_swap.start()
@@ -429,6 +430,16 @@
         @pl.when(has_next)
         def _():
             to_prev[j].wait_recv()
+
+        if j > 0:
+
+            @pl.when(has_prev)
+            def _():
+                home_prev[j - 1].start()
+
+            @pl.when(has_next)
+            def _():
+                home_next[j - 1].start()
 
         for t in range(2):
             spot = edge[t]
@@ -456,9 +467,6 @@
             back[:, :BLOCK] = key_grad.astype(BF16)
             back[:, BLOCK:] = value_grad.astype(BF16)
 
-            @pl.when((has_prev, has_next)[t])
-            def _():
-                (home_prev, home_next)[t][j].start()
 
         own_key = kv[j][:, :BLOCK].astype(F32)
         rolled[j][:BLOCK] = roll_half(own_key[:BLOCK]).astype(BF16)
@@ -507,21 +515,43 @@
                 q_turned[j][s, :, lanes] = turned
                 q_unit[j][s, :, lanes] = unit
 
-    term_dp[dp, 0:1] = jnp.sum(q_term, axis=0, keepdims=True)
-    term_dp[dp, 1:2] = jnp.sum(k_term, axis=0, keepdims=True) / k_gain
-
-    def ctx_copy(step):
-        peer = lax.rem(me + step, n)
-        return remote(term_ctx.at[me], term_ctx.at[me], tc_s.at[step], tc_r.at[step], (dp, peer))
-
-    def dp_copy(step):
+    term_dp[core, dp, 0:1] = jnp.sum(q_term, axis=0, keepdims=True)
+    term_dp[core, dp, 1:2] = jnp.sum(k_term, axis=0, keepdims=True) / k_gain
+
+    gathers = core == 1
+    outer = 2 * pair + 1
+
+    def dp_copy(step, sender):
         peer = lax.rem(dp + step, n_dp)
-        return remote(term_dp.at[dp], term_dp.at[dp], td_s.at[step], td_r.at[step], (peer, me))
-
-    ctx_copies = [ctx_copy(step) for step in range(1, n)]
-    dp_copies = [dp_copy(step) for step in range(1, n_dp)]
-    for copy in dp_copies:
-        copy.start()
+        mine_spot = (core, dp)
+        return remote(
+            term_dp.at[mine_spot],
+            term_dp.at[mine_spot],
+            td_s.at[step],
+            td_r.at[sender, step],
+            (peer, outer),
+        )
+
+    def ctx_copy(step, side):
+        peer = 2 * lax.rem(pair + step, n // 2) + side
+        return remote(
+            term_ctx.at[pair], term_ctx.at[pair], tc_s.at[step, side], tc_r.at[step], (dp, peer)
+        )
+
+    for step in range(1, n_dp):
+        dp_copy(step, core).start()
+
+    @pl.when(jnp.logical_not(gathers))
+    def _():
+        dp_copy(0, 0).start()
+
+    @pl.when(has_prev)
+    def _():
+        home_prev[share - 1].start()
+
+    @pl.when(has_next)
+    def _():
+        home_next[share - 1].start()
 
     for j in range(share):
         for s in (1, 0):
@@ -548,11 +578,17 @@
         ]
         join(j, 1, parts)
 
-    for copy in dp_copies:
-        copy.wait_recv()
-    term_ctx[me, 0:2] = jnp.sum(term_dp[:, 0:2], axis=0)
-    for copy in ctx_copies:
-        copy.start()
+    @pl.when(gathers)
+    def _():
+        for step in range(n_dp):
+            dp_copy(step, 0).wait_recv()
+        for step in range(1, n_dp):
+            dp_copy(step, 1).wait_recv()
+        term_ctx[pair, 0:2] = jnp.sum(jnp.sum(term_dp[:, :, 0:2], axis=0), axis=0)
+        for step in range(1, n // 2):
+            ctx_copy(step, 0).start()
+            ctx_copy(step, 1).start()
+        ctx_copy(0, 0).start()
 
     for j in range(share):
 
@@ -614,20 +650,35 @@
         for other in range(2):
             near_copy(1, other, core).wait_send()
 
-    for copy in dp_copies:
-        copy.wait_send()
+    for step in range(1, n_dp):
+        dp_copy(step, core).wait_send()
+
+    @pl.when(jnp.logical_not(gathers))
+    def _():
+        dp_copy(0, 0).wait_send()
+
     k_home.wait_recv()
     v_home.wait_recv()
     k_home.wait_send()
     v_home.wait_send()
-    for copy in ctx_copies:
-        copy.wait_recv()
+    for step in range(1, n // 2):
+        ctx_copy(step, core).wait_recv()
+
+    @pl.when(jnp.logical_not(gathers))
+    def _():
+        ctx_copy(0, 0).wait_recv()
+
     totals = jnp.sum(term_ctx[:, 0:2], axis=0)
     token_count = n_dp * n * BLOCK
     qgain_ref[...] = totals[0:1] * (1.0 / math.sqrt(token_count * groups * per_group))
     kgain_ref[...] = totals[1:2] * (1.0 / math.sqrt(token_count * groups))
-    for copy in ctx_copies:
-        copy.wait_send()
+
+    @pl.when(gathers)
+    def _():
+        for step in range(1, n // 2):
+            ctx_copy(step, 0).wait_send()
+            ctx_copy(step, 1).wait_send()
+        ctx_copy(0, 0).wait_send()
 
 
 def hand_over(*refs):
@@ -707,8 +758,8 @@
             pltpu.VMEM((share, nat, BLOCK), F32),
             pltpu.VMEM((BLOCK, share * BLOCK), BF16),
             pltpu.VMEM((BLOCK, share * BLOCK), BF16),
-            pltpu.VMEM((n, 8, BLOCK), F32),
-            pltpu.VMEM((n_dp, 8, BLOCK), F32),
+            pltpu.VMEM((n // 2, 8, BLOCK), F32),
+            pltpu.VMEM((2, n_dp, 8, BLOCK), F32),
         ]
         + [pltpu.VMEM((2, BLOCK, wide), BF16)] * (2 * share)
         + [pltpu.VMEM((nat, 2 * BLOCK), BF16)] * share
@@ -730,10 +781,10 @@
             dma((5 + 7 * share,)),
             dma((2, 2)),
             dma((2, 2)),
-            dma((n,)),
-            dma((n,)),
+            dma((n // 2, 2)),
+            dma((n // 2,)),
             dma((n_dp,)),
-            dma((n_dp,)),
+            dma((2, n_dp)),
         ],
         compiler_params=pltpu.CompilerParams(
             collective_id=0, has_side_effects=True, vmem_limit_bytes=VMEM_LIMIT

time: 25 us -> 23.6 us (0.944)
  Pallas kernels: 24.3 us -> 22.8 us
    pallas_call x1, Pallas kernels: 23.2 us -> 21.8 us  [shards(): pl.pallas_call(functools.partial(kernel, n, n_dp, groups, per_group), out...]
where the time goes in v4:
time: 23.6 us; the launch traced here: 23.5 us
  Pallas kernels  22.8 us (97%)
  between operations  0.64 us (3%)
    pallas_call x1, Pallas kernels, shards(): pl.pallas_call(functools.partial(kernel, n, n_dp, groups, per_group), out...  21.8 us
    pallas_call x1, Pallas kernels, shards(): pl.pallas_call(hand_over, out_shape=(pltpu.HBM(q_proj.shape, BF16), pltpu...  1.03 us

profile of v4, /device:TPU:0, one launch (start us, length us, event | category | flops | bytes accessed | tf_op | source)
XLA Modules:
  0.0 23.5 jit_solution(2459447402917702729)
XLA Ops:
  0.6 21.8 %shard_map.146 = (bf16[2,128,1536]{2,1,0:T(8,128)(2,1)S(1)}, bf16[2,128,256]{2,1,0:T(8,128)(2,1)S(1)}, bf16[2,128,256]{2,1,0:T(8,128)(2,1)S(1)}, f32[1,128]{1,0:T(1,128)S(1)}, f32[1,128]{1,0:T(1,128)S(1)}) custom-call(s32[1,8]{1,0:T(1,128)} %refs_0_.1, bf16[1,128,512]{2,1,0:T(8,128)(2,1)} %refs_1_.1, bf16[1,128,512]{2,1,0:T(8,128)(2,1)} %refs_2_.1, ...), custom_call_target="tpu_custom_call" | custom-call | flops 1258291200 | bytes 2359296 | tf_op jit(solution)/shard_map/pallas_call | solution.py:731
  22.5 1.0 %shard_map.147 = (bf16[1,128,3072]{2,1,0:T(8,128)(2,1)}, bf16[1,128,512]{2,1,0:T(8,128)(2,1)}, bf16[1,128,512]{2,1,0:T(8,128)(2,1)}, f32[1,128]{1,0:T(1,128)}, f32[1,128]{1,0:T(1,128)}) custom-call(bf16[2,128,1536]{2,1,0:T(8,128)(2,1)S(1)} %get-tuple-element.15.refs_0_, bf16[2,128,256]{2,1,0:T(8,128)(2,1)S(1)} %get-tuple-element.16.refs_1_, ...), custom_call_target="tpu_custom_call" | custom-call | tf_op jit(solution)/shard_map/pallas_call | solution.py:815

commit v5 on v4

--- a/solution.py
+++ b/solution.py
@@ -180,25 +180,14 @@
     barrier = pltpu.get_barrier_semaphore()
     pl.semaphore_signal(barrier, inc=1, device_id=(dp, partner), device_id_type=MESH)
 
-    def greet_ctx(step, carry):
-        peer = lax.rem(partner + step, n)
-
-        @pl.when(peer != me)
-        def _():
-            pl.semaphore_signal(barrier, inc=1, device_id=(dp, peer), device_id_type=MESH)
-
-        return carry
-
-    def greet_dp(step, carry):
-        peer = lax.rem(dp + step, n_dp)
-        pl.semaphore_signal(barrier, inc=1, device_id=(peer, me), device_id_type=MESH)
-        pl.semaphore_signal(barrier, inc=1, device_id=(peer, partner), device_id_type=MESH)
-        return carry
-
-    lax.fori_loop(1, n, greet_ctx, 0)
-    lax.fori_loop(1, n_dp, greet_dp, 0)
-    for load in loads:
-        load.start()
+    for step in range(1, n // 2):
+        for side in range(2):
+            peer = (dp, 2 * lax.rem(pair + step, n // 2) + side)
+            pl.semaphore_signal(barrier, inc=1, device_id=peer, device_id_type=MESH)
+    for step in range(1, n_dp):
+        for side in range(2):
+            peer = (lax.rem(dp + step, n_dp), 2 * pair + side)
+            pl.semaphore_signal(barrier, inc=1, device_id=peer, device_id_type=MESH)
 
     @pl.when(jnp.logical_not(has_prev))
     def _():
@@ -245,13 +234,20 @@
         numbered(do_hbm.at[0, :, columns(theirs, wide, j)], do_in[j].at[1], partner)
         for j in range(share)
     ]
+    last_block, last_half = slice(2 * BLOCK, 3 * BLOCK), slice(3 * BLOCK, SPAN + BLOCK)
+    first_block, first_half = slice(0, BLOCK), slice(BLOCK, BLOCK + HALF)
+    pieces = [slice(0, BLOCK) if j == 0 else slice(0, 2 * BLOCK) for j in range(share)]
+    values = slice(BLOCK, 2 * BLOCK)
     to_next = [
-        numbered(kv[j].at[2 * BLOCK : 3 * BLOCK], kv[j].at[:BLOCK], me + 2) for j in range(share)
+        numbered(kv[j].at[last_block, pieces[j]], kv[j].at[first_block, pieces[j]], me + 2)
+        for j in range(share)
     ]
     to_prev = [
-        numbered(kv[j].at[BLOCK : BLOCK + HALF], kv[j].at[3 * BLOCK :], me - 2)
+        numbered(kv[j].at[first_half, pieces[j]], kv[j].at[last_half, pieces[j]], me - 2)
         for j in range(share)
     ]
+    ahead_next = numbered(kv[0].at[last_block, values], kv[0].at[first_block, values], me + 2)
+    ahead_prev = numbered(kv[0].at[first_half, values], kv[0].at[last_half, values], me - 2)
     home_prev = [numbered(back_prev[j], arrived[j].at[1], me - 2) for j in range(share)]
     home_next = [numbered(back_next[j], arrived[j].at[0, :HALF], me + 2) for j in range(share)]
     q_home = [
@@ -272,9 +268,11 @@
         )
 
     pl.semaphore_wait(barrier, n - 1 + 2 * (n_dp - 1))
+    v_swap.start()
     ids_swap.start()
     k_swap.start()
-    v_swap.start()
+    for load in loads:
+        load.start()
     for j in range(share):
         q_swap[j].start()
         do_swap[j].start()
@@ -298,6 +296,21 @@
 
     for s in range(2):
         if s == 1:
+            v_swap.wait_recv()
+            for j in range(share):
+                for t in range(2):
+                    spot = slice((1 + t) * BLOCK, (2 + t) * BLOCK)
+                    kv[j][spot, BLOCK:] = v_raw[slot_of[t], :, j * BLOCK : (j + 1) * BLOCK]
+                if j == 0:
+
+                    @pl.when(has_prev)
+                    def _():
+                        ahead_prev.start()
+
+                    @pl.when(has_next)
+                    def _():
+                        ahead_next.start()
+
             ids_swap.wait_recv()
         cosine, sine = rope_tables([ids[s, i] for i in range(3)])
         cosn[s] = cosine
@@ -308,7 +321,6 @@
 
     rolled_k_gain, rolled_q_gain = roll_half(k_gain), roll_half(q_gain)
     k_swap.wait_recv()
-    v_swap.wait_recv()
     for j in range(share):
         lanes = slice(j * BLOCK, (j + 1) * BLOCK)
         for t in range(2):
@@ -318,7 +330,6 @@
             turned = inv * (x * (cosine * k_gain) + roll_half(x) * (sine * rolled_k_gain))
             spot = slice((1 + t) * BLOCK, (2 + t) * BLOCK)
             kv[j][spot, :BLOCK] = turned.astype(BF16)
-            kv[j][spot, BLOCK:] = v_raw[slot_of[t], :, lanes]
             rolled[j][spot] = roll_half(turned).astype(BF16)
 
         @pl.when(has_prev)
@@ -421,6 +432,14 @@
 
     q_term = jnp.zeros((8, BLOCK), F32)
     k_term = jnp.zeros((8, BLOCK), F32)
+    @pl.when(has_prev)
+    def _():
+        ahead_next.wait_recv()
+
+    @pl.when(has_next)
+    def _():
+        ahead_prev.wait_recv()
+
     for j in range(share):
 
         @pl.when(has_prev)
@@ -642,11 +661,13 @@
 
     @pl.when(has_next)
     def _():
+        ahead_next.wait_send()
         for other in range(2):
             near_copy(0, other, core).wait_send()
 
     @pl.when(has_prev)
     def _():
+        ahead_prev.wait_send()
         for other in range(2):
             near_copy(1, other, core).wait_send()
 
@@ -777,8 +798,8 @@
         + [pltpu.VMEM((2, BLOCK, wide), F32)] * (2 * share)
         + [
             dma((9 + 2 * share,)),
-            dma((5 + 7 * share,)),
-            dma((5 + 7 * share,)),
+            dma((7 + 7 * share,)),
+            dma((7 + 7 * share,)),
             dma((2, 2)),
             dma((2, 2)),
             dma((n // 2, 2)),

time: 23.6 us -> 23.3 us (0.987)
  Pallas kernels: 22.8 us -> 22.5 us
    pallas_call x1, Pallas kernels: 21.8 us -> 21.5 us  [shards(): pl.pallas_call(functools.partial(kernel, n, n_dp, groups, per_group), out...]
where the time goes in v5:
time: 23.3 us; the launch traced here: 23.1 us
  Pallas kernels  22.5 us (97%)
  between operations  0.64 us (3%)
    pallas_call x1, Pallas kernels, shards(): pl.pallas_call(functools.partial(kernel, n, n_dp, groups, per_group), out...  21.5 us
    pallas_call x1, Pallas kernels, shards(): pl.pallas_call(hand_over, out_shape=(pltpu.HBM(q_proj.shape, BF16), pltpu...  1.03 us

profile of v5, /device:TPU:0, one launch (start us, length us, event | category | flops | bytes accessed | tf_op | source)
XLA Modules:
  0.0 23.1 jit_solution(15250195548695976727)
XLA Ops:
  0.6 21.5 %shard_map.146 = (bf16[2,128,1536]{2,1,0:T(8,128)(2,1)S(1)}, bf16[2,128,256]{2,1,0:T(8,128)(2,1)S(1)}, bf16[2,128,256]{2,1,0:T(8,128)(2,1)S(1)}, f32[1,128]{1,0:T(1,128)S(1)}, f32[1,128]{1,0:T(1,128)S(1)}) custom-call(s32[1,8]{1,0:T(1,128)} %refs_0_.1, bf16[1,128,512]{2,1,0:T(8,128)(2,1)} %refs_1_.1, bf16[1,128,512]{2,1,0:T(8,128)(2,1)} %refs_2_.1, ...), custom_call_target="tpu_custom_call" | custom-call | flops 1258291200 | bytes 2359296 | tf_op jit(solution)/shard_map/pallas_call | solution.py:752
  22.1 1.0 %shard_map.147 = (bf16[1,128,3072]{2,1,0:T(8,128)(2,1)}, bf16[1,128,512]{2,1,0:T(8,128)(2,1)}, bf16[1,128,512]{2,1,0:T(8,128)(2,1)}, f32[1,128]{1,0:T(1,128)}, f32[1,128]{1,0:T(1,128)}) custom-call(bf16[2,128,1536]{2,1,0:T(8,128)(2,1)S(1)} %get-tuple-element.15.refs_0_, bf16[2,128,256]{2,1,0:T(8,128)(2,1)S(1)} %get-tuple-element.16.refs_1_, ...), custom_call_target="tpu_custom_call" | custom-call | tf_op jit(solution)/shard_map/pallas_call | solution.py:836

commit v6 on v5

--- a/solution.py
+++ b/solution.py
@@ -404,31 +404,18 @@
                     jnp.sum(weights * grad, axis=0, keepdims=True),
                 )
 
-    @pl.when(has_prev)
-    def _():
-        for sender in range(2):
-            near_copy(0, sender, sender).wait_recv()
-
-    @pl.when(has_next)
-    def _():
-        for sender in range(2):
-            near_copy(1, sender, sender).wait_recv()
-
-    before = 1 - lax.rem(plan_ref[0, lax.max(2 * pair - 2, 0)], 2)
-    after = lax.rem(plan_ref[0, lax.min(2 * pair + 2, n - 2)], 2)
-    cosine, sine = rope_tables([near_ids[0, before, i] for i in range(3)])
-    near_cos[:BLOCK] = cosine
-    near_sin[:BLOCK] = sine
-    cosine, sine = rope_tables([near_ids[1, after, i] for i in range(3)])
-    near_cos[BLOCK:] = cosine[:HALF]
-    near_sin[BLOCK:] = sine[:HALF]
-
     def join(j, i, parts):
         even, late = parts
         lanes = slice(i * BLOCK, (i + 1) * BLOCK)
         dkv[j][0, :, lanes] = even[:BLOCK] + late[:BLOCK]
         dkv[j][1, :HALF, lanes] = even[BLOCK:] + late[BLOCK : BLOCK + HALF]
         dkv[j][1, HALF:, lanes] = late[BLOCK + HALF :]
+
+    def edge_values(j, t):
+        grad = jnp.dot(
+            probs_low[j][t][edge[t]], stacked(do_in[j][slot_of[t]]), preferred_element_type=F32
+        )
+        (back_prev, back_next)[t][j][:, BLOCK:] = grad.astype(BF16)
 
     q_term = jnp.zeros((8, BLOCK), F32)
     k_term = jnp.zeros((8, BLOCK), F32)
@@ -476,16 +463,30 @@
             key_grad = (
                 jnp.dot(score_grad[j][t][spot], qrot[j][t], preferred_element_type=F32) * inv_sqrt
             )
-            value_grad = jnp.dot(
-                probs_low[j][t][spot],
-                stacked(do_in[j][slot_of[t]]),
-                preferred_element_type=F32,
-            )
             dk_all[j, shifted(spot, t)] = key_grad
-            back = (back_prev, back_next)[t][j]
-            back[:, :BLOCK] = key_grad.astype(BF16)
-            back[:, BLOCK:] = value_grad.astype(BF16)
-
+            (back_prev, back_next)[t][j][:, :BLOCK] = key_grad.astype(BF16)
+            if j < share - 1:
+                edge_values(j, t)
+
+        if j == 0:
+            @pl.when(has_prev)
+            def _():
+                for sender in range(2):
+                    near_copy(0, sender, sender).wait_recv()
+
+            @pl.when(has_next)
+            def _():
+                for sender in range(2):
+                    near_copy(1, sender, sender).wait_recv()
+
+            before = 1 - lax.rem(plan_ref[0, lax.max(2 * pair - 2, 0)], 2)
+            after = lax.rem(plan_ref[0, lax.min(2 * pair + 2, n - 2)], 2)
+            cosine, sine = rope_tables([near_ids[0, before, i] for i in range(3)])
+            near_cos[:BLOCK] = cosine
+            near_sin[:BLOCK] = sine
+            cosine, sine = rope_tables([near_ids[1, after, i] for i in range(3)])
+            near_cos[BLOCK:] = cosine[:HALF]
+            near_sin[BLOCK:] = sine[:HALF]
 
         own_key = kv[j][:, :BLOCK].astype(F32)
         rolled[j][:BLOCK] = roll_half(own_key[:BLOCK]).astype(BF16)
@@ -564,6 +565,9 @@
     def _():
         dp_copy(0, 0).start()
 
+    for t in range(2):
+        edge_values(share - 1, t)
+
     @pl.when(has_prev)
     def _():
         home_prev[share - 1].start()
@@ -597,6 +601,13 @@
         ]
         join(j, 1, parts)
 
+    k_norm = {}
+    for j in range(share):
+        for s in range(2):
+            x = k_raw[s, :, j * BLOCK : (j + 1) * BLOCK].astype(F32)
+            inv = lax.rsqrt(lane_sums(x * x, ones) * (1.0 / BLOCK) + norm_eps)
+            k_norm[j, s] = (inv, x * inv)
+
     @pl.when(gathers)
     def _():
         for step in range(n_dp):
@@ -625,9 +636,7 @@
             cosine, sine = cosn[s], sinn[s]
             total = dkv[j][t] + arrived[j][t].astype(F32)
             grad = total[:, :BLOCK]
-            x = k_raw[s, :, lanes].astype(F32)
-            inv = lax.rsqrt(lane_sums(x * x, ones) * (1.0 / BLOCK) + norm_eps)
-            unit = x * inv
+            inv, unit = k_norm[j, s]
             turned = grad * cosine - roll_half(grad) * sine
             mean = lane_sums(turned * unit * k_gain, ones) * (1.0 / BLOCK)
             result = (inv * (turned * k_gain - unit * mean)).astype(BF16)

time: 23.3 us -> 23.2 us (level)
  no operation moved by 1% of the time
where the time goes in v6:
time: 23.2 us; the launch traced here: 23 us
  Pallas kernels  22.4 us (97%)
  between operations  0.64 us (3%)
    pallas_call x1, Pallas kernels, shards(): pl.pallas_call(functools.partial(kernel, n, n_dp, groups, per_group), out...  21.4 us
    pallas_call x1, Pallas kernels, shards(): pl.pallas_call(hand_over, out_shape=(pltpu.HBM(q_proj.shape, BF16), pltpu...  1.03 us

profile of v6, /device:TPU:0, one launch (start us, length us, event | category | flops | bytes accessed | tf_op | source)
XLA Modules:
  0.0 23.0 jit_solution(10329679235659749085)
XLA Ops:
  0.6 21.4 %shard_map.146 = (bf16[2,128,1536]{2,1,0:T(8,128)(2,1)S(1)}, bf16[2,128,256]{2,1,0:T(8,128)(2,1)S(1)}, bf16[2,128,256]{2,1,0:T(8,128)(2,1)S(1)}, f32[1,128]{1,0:T(1,128)S(1)}, f32[1,128]{1,0:T(1,128)S(1)}) custom-call(s32[1,8]{1,0:T(1,128)} %refs_0_.1, bf16[1,128,512]{2,1,0:T(8,128)(2,1)} %refs_1_.1, bf16[1,128,512]{2,1,0:T(8,128)(2,1)} %refs_2_.1, ...), custom_call_target="tpu_custom_call" | custom-call | flops 1258291200 | bytes 2359296 | tf_op jit(solution)/shard_map/pallas_call | solution.py:761
  22.0 1.0 %shard_map.147 = (bf16[1,128,3072]{2,1,0:T(8,128)(2,1)}, bf16[1,128,512]{2,1,0:T(8,128)(2,1)}, bf16[1,128,512]{2,1,0:T(8,128)(2,1)}, f32[1,128]{1,0:T(1,128)}, f32[1,128]{1,0:T(1,128)}) custom-call(bf16[2,128,1536]{2,1,0:T(8,128)(2,1)S(1)} %get-tuple-element.15.refs_0_, bf16[2,128,256]{2,1,0:T(8,128)(2,1)S(1)} %get-tuple-element.16.refs_1_, ...), custom_call_target="tpu_custom_call" | custom-call | tf_op jit(solution)/shard_map/pallas_call | solution.py:845

commit v7 on v6

--- a/solution.py
+++ b/solution.py
@@ -615,9 +615,9 @@
         for step in range(1, n_dp):
             dp_copy(step, 1).wait_recv()
         term_ctx[pair, 0:2] = jnp.sum(jnp.sum(term_dp[:, :, 0:2], axis=0), axis=0)
-        for step in range(1, n // 2):
-            ctx_copy(step, 0).start()
-            ctx_copy(step, 1).start()
+        for side in range(2):
+            for step in range(1, n // 2):
+                ctx_copy(step, side).start()
         ctx_copy(0, 0).start()
 
     for j in range(share):

time: 23.2 us -> 23.2 us (level)
  no operation moved by 1% of the time
where the time goes in v7:
time: 23.2 us; the launch traced here: 23 us
  Pallas kernels  22.4 us (97%)
  between operations  0.64 us (3%)
    pallas_call x1, Pallas kernels, shards(): pl.pallas_call(functools.partial(kernel, n, n_dp, groups, per_group), out...  21.4 us
    pallas_call x1, Pallas kernels, shards(): pl.pallas_call(hand_over, out_shape=(pltpu.HBM(q_proj.shape, BF16), pltpu...  1.03 us

profile of v7, /device:TPU:0, one launch (start us, length us, event | category | flops | bytes accessed | tf_op | source)
XLA Modules:
  0.0 23.0 jit_solution(11574898627650132046)
XLA Ops:
  0.6 21.4 %shard_map.146 = (bf16[2,128,1536]{2,1,0:T(8,128)(2,1)S(1)}, bf16[2,128,256]{2,1,0:T(8,128)(2,1)S(1)}, bf16[2,128,256]{2,1,0:T(8,128)(2,1)S(1)}, f32[1,128]{1,0:T(1,128)S(1)}, f32[1,128]{1,0:T(1,128)S(1)}) custom-call(s32[1,8]{1,0:T(1,128)} %refs_0_.1, bf16[1,128,512]{2,1,0:T(8,128)(2,1)} %refs_1_.1, bf16[1,128,512]{2,1,0:T(8,128)(2,1)} %refs_2_.1, ...), custom_call_target="tpu_custom_call" | custom-call | flops 1258291200 | bytes 2359296 | tf_op jit(solution)/shard_map/pallas_call | solution.py:761
  22.0 1.0 %shard_map.147 = (bf16[1,128,3072]{2,1,0:T(8,128)(2,1)}, bf16[1,128,512]{2,1,0:T(8,128)(2,1)}, bf16[1,128,512]{2,1,0:T(8,128)(2,1)}, f32[1,128]{1,0:T(1,128)}, f32[1,128]{1,0:T(1,128)}) custom-call(bf16[2,128,1536]{2,1,0:T(8,128)(2,1)S(1)} %get-tuple-element.15.refs_0_, bf16[2,128,256]{2,1,0:T(8,128)(2,1)S(1)} %get-tuple-element.16.refs_1_, ...), custom_call_target="tpu_custom_call" | custom-call | tf_op jit(solution)/shard_map/pallas_call | solution.py:845
